TPU v7x, 256 devices: a whole 4x4x8 slice. The times are simulated.
256 devices in a mesh: dp: 2 (over y_lo), spatial: 4 (over x), code: 32 (over z, y_hi, core).
Axes of the slice: x: 4, y: 4 (y_hi: 2, y_lo: 2; y = y_hi * 2 + y_lo), z: 8, core: 2. Of those that a mesh axis runs over, the one named last changes fastest.
Arguments:
- features: bfloat16 [8, 16, 16, 512], P('dp', 'spatial'), may hold values from -28 to 28
- conv_weight: bfloat16 [3, 3, 512, 256], replicated, may hold values from -0.09375 to 0.09375
- codebook: float32 [131072, 256], P('code'), may hold values from -1 to 1
- recon_grad: bfloat16 [8, 16, 16, 256], P('dp', 'spatial'), may hold values from -6 to 6
Outputs:
- codebook_grad: float32 [131072, 256], P('code', 'dp')
- feature_grad: bfloat16 [8, 16, 16, 512], P('dp', 'spatial')
All inputs are finite; a program needn't handle non-finite values.
Results may differ from a plain program's by a relative error of at most 0.0065.
Values may be sent and summed in bfloat16 or wider, within the bound.
A program may use at most 128 MiB of HBM per device.

v0:
```python
import jax
import jax.numpy as jnp
from jax import lax
from jax.sharding import PartitionSpec as P


def with_halo(x, sides, width):
    for axis, dim in sides:
        peers, length = (lax.axis_size(axis), x.shape[dim])
        up = [(i, (i + 1) % peers) for i in range(peers - 1)]
        down = [(j, i) for i, j in up]
        last = lax.slice_in_dim(x, length - width, length, axis=dim)
        first = lax.slice_in_dim(x, 0, width, axis=dim)
        before = lax.ppermute(last, axis, up)
        after = lax.ppermute(first, axis, down)
        x = jnp.concatenate([before, x, after], axis=dim)
    return x


def convolve_band(inputs, kernel):
    return lax.conv_general_dilated(
        inputs,
        kernel,
        (1, 1),
        ((0, 0), (1, 1)),
        dimension_numbers=("NHWC", "HWIO", "NHWC"),
        preferred_element_type=jnp.float32,
    )


def make_payload(weights, codebook):
    highest = lax.Precision.HIGHEST
    partial_value = jnp.dot(weights, codebook, precision=highest)
    return partial_value


def on_device(features, conv_weight, codebook, recon_grad):
    highest = lax.Precision.HIGHEST
    padded = with_halo(features, (("spatial", 1),), 1)
    latent = convolve_band(padded, conv_weight)
    feature_width = latent.shape[-1]
    latent_rows = latent.reshape(-1, feature_width)
    upstream = recon_grad.reshape(-1, feature_width).astype(jnp.float32)
    scores = jnp.dot(latent_rows, codebook.T, precision=highest)
    projected = jnp.dot(upstream, codebook.T, precision=highest)
    top_score = lax.pmax(jnp.max(scores, axis=1), "code")
    weights = jnp.exp(scores - top_score[:, None])
    payload = make_payload(weights, codebook)
    mass_total, summed = lax.psum((jnp.sum(weights, axis=1), payload), "code")
    reconstructed = summed[:, :feature_width] / mass_total[:, None]
    inner_dot = jnp.sum(upstream * reconstructed, axis=1)
    probabilities = jnp.exp(scores - top_score[:, None]) / mass_total[:, None]
    grad_scores = probabilities * (projected - inner_dot[:, None])
    latent_total = lax.psum(jnp.dot(grad_scores, codebook, precision=highest), "code")
    latent_grad = latent_total.astype(jnp.bfloat16).reshape(latent.shape)
    code_terms = jnp.dot(probabilities.T, upstream, precision=highest) + jnp.dot(
        grad_scores.T, latent_rows, precision=highest
    )
    entries_all = codebook.shape[0] * lax.axis_size("code")
    rows_all = latent_rows.shape[0] * lax.axis_size("dp") * lax.axis_size("spatial")
    grad_factor = entries_all / rows_all
    reduced = lax.psum(code_terms, ("dp", "spatial"))
    column_width = feature_width // lax.axis_size("dp")
    own_block = lax.dynamic_slice_in_dim(
        reduced, lax.axis_index("dp") * column_width, column_width, 1
    )
    codebook_grad = own_block * grad_factor
    extended = with_halo(latent_grad, (("spatial", 1),), 1)
    flipped = jnp.transpose(conv_weight[::-1, ::-1], (0, 1, 3, 2))
    feature_grad = convolve_band(extended, flipped).astype(jnp.bfloat16)
    return (codebook_grad, feature_grad)


def solution(mesh):
    placed = (P("dp", "spatial", None, None), P(), P("code", None), P("dp", "spatial", None, None))
    return jax.shard_map(
        on_device,
        mesh=mesh,
        in_specs=placed,
        out_specs=(P("code", "dp"), P("dp", "spatial", None, None)),
        check_vma=False,
    )
```

profile of v0, /device:TPU:1, one launch (start us, length us, event | category | flops | bytes accessed | tf_op | source)
XLA Modules:
  0.0 664.5 jit_solution(6463394012962144440)
XLA Ops:
  7.2 0.0 copy-start
  7.2 0.0 copy-start.6
  7.2 0.0 all-reduce.4.cloned.1.call-start
  7.2 1.0 fusion.16
  8.3 3.9 collective-permute-start
  12.2 1.3 collective-permute-start.1
  13.5 0.0 collective-permute-done
  13.5 3.7 collective-permute-done.1
  17.2 1.0 maximum_bitcast_fusion
  18.2 0.3 copy.20
  18.6 0.2 pad.clone
  18.8 0.1 slice.20
  18.9 0.4 fusion.7
  19.3 0.0 copy-done
  19.3 0.0 copy-done.6
  19.3 0.0 copy-start.1
  19.4 1.1 convolution_select_fusion.1
  20.4 0.3 copy.12
  20.8 0.7 copy-done.1
  21.5 5.4 fusion.18
  26.9 69.7 %pmax.7 = f32[256]{0:T(256)S(1)} all-reduce(f32[256]{0:T(256)S(1)} %get-tuple-element.8), channel_id=1, replica_groups=mesh['dp'=2,'spatial'=4,'code'=32] {'code'}, use_global_device_ids=true, to_apply=%region_1.0 | all-reduce | flops 256 | bytes 2048 | tf_op jit(solution)/shard_map/pmax | solution.py:46
  96.6 0.0 copy-start.2
  96.6 3.0 fusion.3
  99.7 0.4 copy-done.2
  100.1 0.0 copy-start.5
  100.1 6.9 %fusion.1 = f32[256,256]{1,0:T(8,128)} fusion(f32[4096,256]{1,0:T(8,128)S(1)} %copy-done.2, f32[256,4096]{1,0:T(8,128)} %get-tuple-element.9, f32[256]{0:T(256)S(1)} %pmax.7), kind=kOutput, calls=%fused_computation.4 | convolution fusion | flops 3222274048 | bytes 8651776 | tf_op jit(solution)/shard_map/dot_general | solution.py:33
  107.0 68.2 %psum.28 = f32[256]{0:T(256)S(1)} all-reduce(f32[256]{0:T(256)S(1)} %fusion.3), channel_id=1, replica_groups=mesh['dp'=2,'spatial'=4,'code'=32] {'code'}, use_global_device_ids=true, to_apply=%region_3.0 | all-reduce | flops 256 | bytes 2048 | tf_op jit(solution)/shard_map/psum | solution.py:49
  175.3 0.0 all-reduce.4.cloned.1.call-update
  175.3 0.2 all-reduce.6.cloned.1.call-start
  175.5 0.0 copy-done.5
  175.5 7.8 %fusion.14 = f32[4096,256]{1,0:T(8,128)} fusion(bf16[256,256]{1,0:T(8,128)(2,1)S(1)} %bitcast.43, f32[256,4096]{1,0:T(8,128)} %get-tuple-element.9, f32[256]{0:T(256)S(1)} %psum.28, f32[256]{0:T(256)S(1)} %pmax.7), kind=kOutput, calls=%fused_computation.27 | convolution fusion | flops 3223322624 | bytes 8521728 | tf_op jit(solution)/shard_map/dot_general | solution.py:56
  183.3 252.9 %all-reduce.4.cloned.1.call-done = f32[256,256]{1,0:T(8,128)} async-done(((f32[256,256]{1,0:T(8,128)}), f32[256,256]{1,0:T(8,128)}) %all-reduce.4.cloned.1.call-update) | async-done | bytes 262160 | tf_op jit(solution)/shard_map/psum | solution.py:49
  436.2 1.1 multiply_reduce_fusion
  437.3 0.0 copy-start.4
  437.3 6.8 %fusion = f32[256,4096]{1,0:T(8,128)S(1)} fusion(bf16[256,256]{1,0:T(8,128)(2,1)S(1)} %bitcast.44, f32[4096,256]{1,0:T(8,128)} %param.6, f32[256]{0:T(256)S(1)} %multiply_reduce_fusion, f32[256]{0:T(256)S(1)} %psum.28, f32[256,4096]{1,0:T(8,128)} %get-tuple-element.9, f32[256]{0:T(256)S(1)} %pmax.7), kind=kOutput, calls=%fused_computation.2 | convolution fusion | flops 3225419776 | bytes 12717056 | tf_op jit(solution)/shard_map/dot_general | solution.py:45
  444.1 0.0 copy-start.3
  444.1 1.9 copy-done.3
  446.0 0.0 copy-done.4
  446.0 8.2 %convolution_add_fusion = f32[4096,256]{1,0:T(8,128)} fusion(f32[4096,256]{1,0:T(8,128)S(1)} %copy-done.4, f32[256,4096]{1,0:T(8,128)S(1)} %fusion, f32[256,256]{1,0:T(8,128)S(1)} %bitcast.37), kind=kOutput, calls=%fused_computation | convolution fusion | flops 3222274048 | bytes 12845056 | tf_op jit(solution)/shard_map/dot_general | solution.py:56
  454.2 0.0 all-reduce.6.cloned.1.call-update
  454.2 7.1 %fusion.19 = f32[256,256]{1,0:T(8,128)S(1)} fusion(f32[256,4096]{1,0:T(8,128)} %copy-done.3, f32[4096,256]{1,0:T(8,128)} %param.6), kind=kOutput, calls=%fused_computation.31 | convolution fusion | flops 3221225472 | bytes 8650752 | tf_op jit(solution)/shard_map/dot_general | solution.py:54
  461.3 184.3 %all-reduce.7 = bf16[256,256]{1,0:T(8,128)(2,1)S(1)} all-reduce(f32[256,256]{1,0:T(8,128)S(1)} %fusion.19), channel_id=1, replica_groups=mesh['dp'=2,'spatial'=4,'code'=32] {'code'}, use_global_device_ids=true, to_apply=%region_7.0 | all-reduce | flops 65536 | bytes 393216 | tf_op jit(solution)/shard_map/psum | solution.py:54
  645.6 0.1 copy.14
  645.8 1.3 collective-permute-start.2
  647.1 1.3 collective-permute-start.3
  648.4 0.0 collective-permute-done.2
  648.4 3.3 collective-permute-done.3
  651.7 0.1 maximum_bitcast_fusion.1
  651.9 0.1 pad.2
  652.0 0.1 slice.24
  652.1 0.2 fusion.11
  652.3 1.1 fusion.6
  653.4 0.3 copy.18
  653.7 0.1 slice_bitcast_fusion
  653.8 0.8 copy.19
  654.6 0.0 all-reduce.6.cloned.1.call-done
  654.6 3.0 dynamic-slice_multiply_fusion
  (3 shorter events, 0.1 us)
Async XLA Ops:
  7.2 12.2 %copy-start = (bf16[3,3,512,256]{3,2,1,0:T(8,128)(2,1)S(1)}, bf16[3,3,512,256]{3,2,1,0:T(8,128)(2,1)}, u32[]{:S(2)}) copy-start(bf16[3,3,512,256]{3,2,1,0:T(8,128)(2,1)} %param.5) | copy-start | bytes 7077892
  7.2 12.2 %copy-start.6 = (pred[32,3]{0,1:T(4,128)(4,1)S(1)}, pred[32,3]{0,1:T(4,128)(4,1)}, u32[]{:S(2)}) copy-start(pred[32,3]{0,1:T(4,128)(4,1)} %constant.26) | copy-start | bytes 292
  7.2 429.0 %all-reduce.4.cloned.1.call-start = ((), (), s32[]{:S(2)}) async-start(), calls=%async_computation | async-start | bytes 524288 | tf_op jit(solution)/shard_map/psum | solution.py:49
  8.3 5.3 collective-permute-start
  12.2 5.0 collective-permute-start.1
  19.3 2.2 copy-start.1
  96.6 3.4 copy-start.2
  100.1 75.5 %copy-start.5 = (bf16[4,4,16,256]{3,2,1,0:T(8,128)(2,1)S(1)}, bf16[4,4,16,256]{3,2,1,0:T(8,128)(2,1)}, u32[]{:S(2)}) copy-start(bf16[4,4,16,256]{3,2,1,0:T(8,128)(2,1)} %param.7) | copy-start | bytes 393220
  175.3 479.3 %all-reduce.6.cloned.1.call-start = ((), (), s32[]{:S(2)}) async-start(), calls=%async_computation.1 | async-start | bytes 8388608 | tf_op jit(solution)/shard_map/psum | solution.py:62
  437.3 8.7 %copy-start.4 = (f32[4096,256]{1,0:T(8,128)S(1)}, f32[4096,256]{1,0:T(8,128)}, u32[]{:S(2)}) copy-start(f32[4096,256]{1,0:T(8,128)} %fusion.14) | copy-start | bytes 12582916
  444.1 1.9 copy-start.3
  645.8 2.6 collective-permute-start.2
  647.1 4.7 collective-permute-start.3
Sparse Core Ops, SparseCore 0:
  175.4 260.7 all-reduce.3
  454.4 109.7 all-reduce.5
where the time goes:
time: 670 us; the launch traced here: 664 us
  blocking collectives  322 us (48%)
  waiting for transfers between devices  260 us (39%)
  matrix products  44.3 us (7%)
  between operations  14.3 us (2%)
  other arithmetic  9 us (1%)
  starting transfers between devices  8.08 us (1%)
    psum x1, waiting for transfers between devices, on_device(): mass_total, summed = lax.psum((jnp.sum(weights, axis=1), payload), 'code')  253 us
    psum x1, blocking collectives, on_device(): lax.psum(jnp.dot(grad_scores, codebook, precision=highest), 'code')  184 us
    pmax x1, blocking collectives, on_device(): top_score = lax.pmax(jnp.max(scores, axis=1), 'code')  69.7 us
    psum x1, blocking collectives, on_device(): mass_total, summed = lax.psum((jnp.sum(weights, axis=1), payload), 'code')  68.2 us
  transfers between devices with their start and end apart: 6, of which 3 were waited for; matrix products, arithmetic and copies ran while one was open for 3% of the time, Pallas kernels for 0%

commit v1 on v0

v1 whole, which is shorter than its diff:
```python
import functools

import jax
import jax.numpy as jnp
from jax import lax
from jax.experimental import pallas as pl
from jax.experimental.pallas import tpu as pltpu
from jax.sharding import PartitionSpec as P

MESH = pl.DeviceIdType.MESH
BF = jnp.bfloat16
F32 = jnp.float32
NX, NY, NZ = 4, 4, 8
IMG, BAND, LW, CIN, D = 4, 4, 16, 512, 256
ROWS = IMG * BAND * LW
CODES = 4096
HALF = CODES // 2
BLK = HALF // NX
OWN = IMG * BAND * LW // 4
HD = D // 2
EDGE_SEMS = 8


def nt(a, b):
    return lax.dot_general(a, b, (((1,), (1,)), ((), ())), preferred_element_type=F32)


def nn(a, b):
    return lax.dot_general(a, b, (((1,), (0,)), ((), ())), preferred_element_type=F32)


def tn(a, b):
    return lax.dot_general(a, b, (((0,), (0,)), ((), ())), preferred_element_type=F32)


def shifted(acc, step):
    rows = acc.shape[0]
    col = lax.broadcasted_iota(jnp.int32, acc.shape, 0) % LW
    keep = (col >= 1) if step == 1 else (col < LW - 1)
    return jnp.where(keep, pltpu.roll(acc, step % rows, 0), 0.0)


def kernel(
    feat, cw_hbm, cb_hbm, up,
    cg, fg,
    xp, cw, cb, hi, lo, right, lat_lo, wts, proj, mst, pg, gb,
    st, st_col, st_z, snd, rcv, own, fin,
    gsum, g_col, gz_src, g_z, lg_src, lg,
    l_sem, h_ss, h_rs, u_ss, u_rs, t_ss, t_rs, sc_ss, sc_rs, sz_ss, sz_rs,
    r_ss, r_rs, a_ss, a_rs, gc_ss, gc_rs, gz_ss, gz_rs, lg_ss, lg_rs, e_ss, e_rs,
):
    d, s, k = lax.axis_index("dp"), lax.axis_index("spatial"), lax.axis_index("code")
    z, yh, c = k // 4, (k // 2) % 2, k % 2
    y = yh * 2 + d

    def dev(x_, y_, z_, c_):
        return (y_ % 2, x_, z_ * 4 + (y_ // 2) * 2 + c_)

    def xdev(o):
        return dev((s + o) % NX, y, z, c)

    def ydev(j):
        return dev(s, (y + j) % NY, z, c)

    def coldev(i):
        return dev(s, (y + i // 2) % NY, z, (c + i) % 2)

    def zdev(i):
        return dev(s, y, (z + i) % NZ, c)

    def agdev(f, o):
        return ((d + f) % 2, (s + o) % NX, k)

    def edgedev(e, i):
        return dev((s + e) % NX, (y + 2 * (i // 2)) % NY, z, (c + i) % 2)

    def remote(src, dst, ss, rs, who):
        return pltpu.make_async_remote_copy(
            src_ref=src, dst_ref=dst, send_sem=ss, recv_sem=rs,
            device_id=who, device_id_type=MESH,
        )

    load_cb = pltpu.make_async_copy(cb_hbm.at[pl.ds(d * HALF, HALF)], cb, l_sem.at[0])
    load_u = pltpu.make_async_copy(up, right.at[pl.ds(0, ROWS)], l_sem.at[1])
    load_x = pltpu.make_async_copy(feat, xp.at[:, pl.ds(1, BAND)], l_sem.at[2])
    load_w = pltpu.make_async_copy(cw_hbm, cw, l_sem.at[3])
    barrier = pltpu.get_barrier_semaphore()
    peers = [xdev(o) for o in range(1, NX)] + [coldev(i) for i in range(1, 8)]
    peers += [zdev(i) for i in range(1, NZ)] + [agdev(1, o) for o in range(1, NX)]
    peers += [edgedev(e, i) for e in (1, NX - 1) for i in range(1, 4)]
    for who in peers:
        pl.semaphore_signal(barrier, inc=1, device_id=who, device_id_type=MESH)
    load_cb.start()
    load_u.start()
    load_x.start()
    load_w.start()
    load_cb.wait()

    @pl.loop(0, HALF // 256)
    def _(i):
        rows = pl.ds(pl.multiple_of(i * 256, 256), 256)
        v = cb[rows, :]
        h = v.astype(BF)
        hi[rows, :] = h
        lo[rows, :] = (v - h.astype(F32)).astype(BF)

    pl.semaphore_wait(barrier, len(peers))

    halo = [
        remote(feat.at[:, BAND - 1], xp.at[:, 0], h_ss.at[0], h_rs.at[0], xdev(1)),
        remote(feat.at[:, 0], xp.at[:, BAND + 1], h_ss.at[1], h_rs.at[1], xdev(NX - 1)),
    ]
    hrows = ROWS // 2
    give_u = [
        remote(
            up.at[pl.ds(n * hrows, hrows)], right.at[pl.ds(ROWS + n * hrows, hrows)],
            u_ss.at[n], u_rs.at[n], ydev((1, 3)[n]),
        )
        for n in range(2)
    ]
    for cp in halo + give_u:
        cp.start()

    def project(rb):
        u = right[rb * ROWS:(rb + 1) * ROWS, :]

        @pl.loop(0, NX)
        def _(i):
            rows = pl.ds(pl.multiple_of(i * BLK, BLK), BLK)
            proj[rows, rb * ROWS:(rb + 1) * ROWS] = nt(hi[rows, :], u) + nt(lo[rows, :], u)

    load_u.wait()
    project(0)

    load_x.wait()
    load_w.wait()
    for cp in halo:
        cp.wait_recv()

    @pl.when(s == 0)
    def _():
        xp[:, 0] = jnp.zeros((IMG, LW, CIN), BF)

    @pl.when(s == NX - 1)
    def _():
        xp[:, BAND + 1] = jnp.zeros((IMG, LW, CIN), BF)

    def taps(b):
        acc = None
        for a in range(3):
            xa = xp[:, a:a + BAND].reshape(ROWS, CIN)
            t = nn(xa, cw[a, b])
            acc = t if acc is None else acc + t
        return acc

    latent = taps(1) + shifted(taps(0), 1) + shifted(taps(2), -1)
    lat_hi = latent.astype(BF)
    right[2 * ROWS:3 * ROWS, :] = lat_hi
    lat_lo[:ROWS, :] = (latent - lat_hi.astype(F32)).astype(BF)
    give_t = []
    for n in range(2):
        rows = pl.ds(2 * ROWS + n * hrows, hrows)
        to = pl.ds(3 * ROWS + n * hrows, hrows)
        give_t.append(remote(right.at[rows], right.at[to], t_ss.at[n], t_rs.at[n], ydev((1, 3)[n])))
        rows = pl.ds(n * hrows, hrows)
        to = pl.ds(ROWS + n * hrows, hrows)
        give_t.append(remote(lat_lo.at[rows], lat_lo.at[to], t_ss.at[2 + n], t_rs.at[2 + n], ydev((1, 3)[n])))
    for cp in give_t:
        cp.start()

    def merge(a, b):
        top = jnp.maximum(a[0], b[0])
        ea, eb = jnp.exp(a[0] - top), jnp.exp(b[0] - top)
        return top, a[1] * ea + b[1] * eb, a[2] * ea + b[2] * eb

    def score(rb):
        cols = slice(rb * ROWS, (rb + 1) * ROWS)
        lh = right[(2 + rb) * ROWS:(3 + rb) * ROWS, :]
        ll = lat_lo[cols, :]

        def step(i, carry):
            rows = pl.ds(pl.multiple_of(i * BLK, BLK), BLK)
            h = hi[rows, :]
            sc = nt(h, lh) + (nt(h, ll) + nt(lo[rows, :], lh))
            top = jnp.max(sc, axis=0, keepdims=True)
            w = jnp.exp(sc - top)
            wts[rows, cols] = w
            mst[i, :, cols] = top
            mass = jnp.sum(w, axis=0, keepdims=True)
            dots = jnp.sum(w * proj[rows, cols], axis=0, keepdims=True)
            return merge(carry, (top, mass, dots))

        zero = jnp.zeros((1, ROWS), F32)
        top, mass, dots = lax.fori_loop(0, NX, step, (zero - 3.0e38, zero, zero))
        logs, mean = top + jnp.log(mass), dots / mass
        for n in range(2):
            st[2 * rb + n:2 * rb + n + 1, :] = logs[:, n * 128:(n + 1) * 128]
            st[4 + 2 * rb + n:5 + 2 * rb + n, :] = mean[:, n * 128:(n + 1) * 128]

    score(0)
    for cp in give_u:
        cp.wait_recv()
    project(1)
    for cp in give_t:
        cp.wait_recv()
    score(1)

    def combine(parts):
        top = functools.reduce(jnp.maximum, [p[:4] for p in parts])
        mass, dots = 0.0, 0.0
        for p in parts:
            e = jnp.exp(p[:4] - top)
            mass, dots = mass + e, dots + e * p[4:]
        return top + jnp.log(mass), dots / mass

    def swap(p):
        return jnp.concatenate([p[2:4], p[0:2], p[6:8], p[4:6]], axis=0)

    col = [remote(st, st_col.at[i - 1], sc_ss.at[i - 1], sc_rs.at[i - 1], coldev(i)) for i in range(1, 8)]
    for cp in col:
        cp.start()
    for cp in col:
        cp.wait_recv()
    parts = [st[...]]
    for i in range(1, 8):
        p = st_col[i - 1]
        parts.append(swap(p) if (i // 2) % 2 else p)
    logs, mean = combine(parts)
    st_z[0] = jnp.concatenate([logs, mean], axis=0)
    zs = [remote(st_z.at[0], st_z.at[i], sz_ss.at[i - 1], sz_rs.at[i - 1], zdev(i)) for i in range(1, NZ)]
    for cp in zs:
        cp.start()
    for cp in zs:
        cp.wait_recv()
    logs, mean = combine([st_z[i] for i in range(NZ)])
    total = jnp.concatenate([logs[n:n + 1] for n in range(4)], axis=1)
    inner = jnp.concatenate([mean[n:n + 1] for n in range(4)], axis=1)

    both = 2 * ROWS
    sums = []
    for o in (2, 1, 3, 0):
        blk = (s + o) % NX
        rows = pl.ds(pl.multiple_of(blk * BLK, BLK), BLK)
        p = wts[rows, :] * jnp.exp(mst[blk] - total)
        g = (p * (proj[rows, :] - inner)).astype(BF)
        pg[:, :both] = p.astype(BF)
        pg[:, both:] = g
        gb[rows, :] = g
        term = nn(pg[...], right[...])
        if o:
            snd[o - 1] = term.astype(BF)
            cp = remote(snd.at[o - 1], rcv.at[o - 1], r_ss.at[o - 1], r_rs.at[o - 1], xdev(o))
            cp.start()
            sums.append(cp)
        else:
            own[...] = term

    gsum[...] = tn(gb[...], hi[...]).astype(BF)

    def image(y_, c_):
        return (y_ // 2) * 2 + c_

    gcol = []
    for i in range(1, 8):
        j = i // 2
        base = (j % 2) * ROWS + image((y + j) % NY, (c + i) % 2) * OWN
        rows = pl.ds(pl.multiple_of(base, OWN), OWN)
        gcol.append(remote(gsum.at[rows], g_col.at[i - 1], gc_ss.at[i - 1], gc_rs.at[i - 1], coldev(i)))
    for cp in gcol:
        cp.start()
    for cp in gcol:
        cp.wait_recv()
    img = image(y, c)
    part = gsum[pl.ds(pl.multiple_of(img * OWN, OWN), OWN), :].astype(F32)
    for i in range(7):
        part = part + g_col[i].astype(F32)
    gz_src[...] = part.astype(BF)
    gzs = [remote(gz_src, g_z.at[i - 1], gz_ss.at[i - 1], gz_rs.at[i - 1], zdev(i)) for i in range(1, NZ)]
    for cp in gzs:
        cp.start()

    for cp in sums:
        cp.wait_recv()
    block = own[...]
    for o in range(3):
        block = block + rcv[o].astype(F32)
    left, rest = block[:, :HD].astype(BF), block[:, HD:].astype(BF)
    fin[0] = jnp.where(d == 0, left, rest)
    fin[1] = jnp.where(d == 0, rest, left)
    place = cg.at[pl.ds(pl.multiple_of(d * HALF + s * BLK, BLK), BLK)]
    out = []
    for f in (0, 1):
        for o in (2, 1, 3, 0):
            if f or o:
                n = f * NX + o
                out.append(remote(fin.at[f], place, a_ss.at[n], a_rs.at[n], agdev(f, o)))
    for cp in out:
        cp.start()
    keep = pltpu.make_async_copy(fin.at[0], place, l_sem.at[4])
    keep.start()

    for cp in gzs:
        cp.wait_recv()
    for i in range(NZ - 1):
        part = part + g_z[i].astype(F32)
    lg_src[...] = part.astype(BF).reshape(BAND, LW, D)
    lg[img, pl.ds(1, BAND)] = lg_src[...]
    back = []
    for n, i in enumerate((1, 4, 5)):
        back.append(remote(lg_src, lg.at[img, pl.ds(1, BAND)], lg_ss.at[n], lg_rs.at[n], coldev(i)))
    for n, (e, edge, to) in enumerate(((1, BAND - 1, 0), (NX - 1, 0, BAND + 1))):
        for i in range(4):
            m = n * 4 + i
            back.append(remote(lg_src.at[edge], lg.at[img, to], e_ss.at[m], e_rs.at[m], edgedev(e, i)))
    for cp in back:
        cp.start()
    for cp in back:
        cp.wait_recv()

    @pl.when(s == 0)
    def _():
        lg[:, 0] = jnp.zeros((IMG, LW, D), BF)

    @pl.when(s == NX - 1)
    def _():
        lg[:, BAND + 1] = jnp.zeros((IMG, LW, D), BF)

    def back_taps(b):
        acc = None
        for a in range(3):
            la = lg[:, 2 - a:2 - a + BAND].reshape(ROWS, D)
            t = nt(la, cw[a, b])
            acc = t if acc is None else acc + t
        return acc

    grad = back_taps(1) + shifted(back_taps(0), -1) + shifted(back_taps(2), 1)
    fg[...] = grad.astype(BF).reshape(IMG, BAND, LW, CIN)

    for cp in halo + give_u + give_t + col + zs + sums + gcol + gzs + back:
        cp.wait_send()
    keep.wait()
    for cp in out:
        cp.wait()


def on_device(features, conv_weight, codebook, recon_grad):
    dma = pltpu.SemaphoreType.DMA
    vm = pltpu.VMEM
    hbm = pl.BlockSpec(memory_space=pl.ANY)
    sems = [5, 2, 2, 2, 2, 4, 4, 7, 7, 7, 7, 3, 3, 8, 8, 7, 7, 7, 7, 3, 3, 8, 8]
    cg, fg = pl.pallas_call(
        kernel,
        out_shape=(
            jax.ShapeDtypeStruct((CODES, HD), BF),
            jax.ShapeDtypeStruct((IMG, BAND, LW, CIN), BF),
        ),
        in_specs=[hbm] * 4,
        out_specs=(hbm, pl.BlockSpec(memory_space=pltpu.VMEM)),
        scratch_shapes=[
            vm((IMG, BAND + 2, LW, CIN), BF),
            vm((3, 3, CIN, D), BF),
            vm((HALF, D), F32),
            vm((HALF, D), BF),
            vm((HALF, D), BF),
            vm((4 * ROWS, D), BF),
            vm((2 * ROWS, D), BF),
            vm((HALF, 2 * ROWS), F32),
            vm((HALF, 2 * ROWS), F32),
            vm((NX, 1, 2 * ROWS), F32),
            vm((BLK, 4 * ROWS), BF),
            vm((HALF, 2 * ROWS), BF),
            vm((8, 128), F32),
            vm((7, 8, 128), F32),
            vm((NZ, 8, 128), F32),
            vm((3, BLK, D), BF),
            vm((3, BLK, D), BF),
            vm((BLK, D), F32),
            vm((2, BLK, HD), BF),
            vm((2 * ROWS, D), BF),
            vm((7, OWN, D), BF),
            vm((OWN, D), BF),
            vm((NZ - 1, OWN, D), BF),
            vm((BAND, LW, D), BF),
            vm((IMG, BAND + 2, LW, D), BF),
        ] + [dma((n,)) for n in sems],
        compiler_params=pltpu.CompilerParams(
            collective_id=0, has_side_effects=True, vmem_limit_bytes=56 << 20
        ),
        cost_estimate=pl.CostEstimate(
            flops=12 * 2**30, bytes_accessed=10 << 20, transcendentals=1 << 21
        ),
        name="soft_quantize",
    )(features, conv_weight, codebook, recon_grad.reshape(ROWS, D))
    entries_all = codebook.shape[0] * lax.axis_size("code")
    rows_all = ROWS * lax.axis_size("dp") * lax.axis_size("spatial")
    return cg.astype(F32) * (entries_all / rows_all), fg


def solution(mesh):
    placed = (P("dp", "spatial", None, None), P(), P("code", None), P("dp", "spatial", None, None))
    return jax.shard_map(
        on_device,
        mesh=mesh,
        in_specs=placed,
        out_specs=(P("code", "dp"), P("dp", "spatial", None, None)),
        check_vma=False,
    )
```

time: 670 us -> 69.8 us (0.10)
  blocking collectives: 322 us -> 0 us
  waiting for transfers between devices: 260 us -> 0 us
  Pallas kernels: 0 us -> 65.6 us
  matrix products: 44.3 us -> 0 us
  between operations: 14.3 us -> 0.65 us
  starting transfers between devices: 8.08 us -> 0 us
    psum x2 -> x0, waiting for transfers between devices: 253 us -> none  [the longest x1 253 us: on_device(): mass_total, summed = lax.psum((jnp.sum(weights, axis=1), payload), 'code')]
    psum x2 -> x0, blocking collectives: 253 us -> none  [the longest x1 184 us: on_device(): lax.psum(jnp.dot(grad_scores, codebook, precision=highest), 'code')]
    pmax x1 -> x0, blocking collectives: 69.7 us -> none  [on_device(): top_score = lax.pmax(jnp.max(scores, axis=1), 'code')]
    pallas_call x0 -> x1, Pallas kernels: none -> 65.6 us  [on_device(): pl.pallas_call(kernel, out_shape=(jax.ShapeDtypeStruct((CODES, HD), BF),...]
    dot_general x6 -> x0, matrix products: 42.1 us -> none  [the longest x1 8.2 us: on_device(): jnp.dot(grad_scores.T, latent_rows, precision=highest)]
    ppermute x4 -> x0, starting transfers between devices: 7.82 us -> none  [the longest x2 5.24 us: with_halo(): before = lax.ppermute(last, axis, up)]
    ppermute x4 -> x0, waiting for transfers between devices: 7.06 us -> none  [the longest x2 7.04 us: with_halo(): after = lax.ppermute(first, axis, down)]
  transfers between devices with their start and end apart: 6 -> 0, of which waited for: 3 -> 0; matrix products, arithmetic and copies ran while one was open for 3% -> 0% of each run, Pallas kernels for 0% -> 0%
where the time goes in v1:
time: 69.8 us; the launch traced here: 69.7 us
  Pallas kernels  65.6 us (94%)
  other arithmetic  2.72 us (4%)
  local copies, waits for them, and re-layouts  0.71 us (1%)
    pallas_call x1, Pallas kernels, on_device(): pl.pallas_call(kernel, out_shape=(jax.ShapeDtypeStruct((CODES, HD), BF),...  65.6 us
    mul x1, other arithmetic, on_device(): return (cg.astype(F32) * (entries_all / rows_all), fg)  2.72 us

profile of v1, /device:TPU:1, one launch (start us, length us, event | category | flops | bytes accessed | tf_op | source)
XLA Modules:
  0.0 69.7 jit_solution(14754730332069979911)
XLA Ops:
  0.6 65.6 %soft_quantize.1 = (bf16[4096,128]{1,0:T(8,128)(2,1)}, bf16[4,4,16,512]{3,2,1,0:T(8,128)(2,1)}) custom-call(bf16[4,4,16,512]{3,2,1,0:T(8,128)(2,1)} %feat.1, bf16[3,3,512,256]{3,2,1,0:T(8,128)(2,1)} %cw_hbm.1, f32[4096,256]{1,0:T(8,128)} %cb_hbm.1, bf16[256,256]{1,0:T(8,128)(2,1)} %bitcast.1), custom_call_target="tpu_custom_call" | custom-call | flops 12884901888 | bytes 10485760 | tf_op jit(solution)/shard_map/soft_quantize/pallas_call | solution.py:351
  66.2 0.0 copy-start
  66.2 2.7 %convert_multiply_fusion = f32[4096,128]{1,0:T(8,128)} fusion(bf16[4096,128]{1,0:T(8,128)(2,1)} %get-tuple-element.4), kind=kLoop, calls=%fused_computation | loop fusion | flops 1048576 | bytes 3145728 | tf_op jit(solution)/shard_map/mul | solution.py:396
  69.0 0.0 copy-done
  69.0 0.7 %copy.7 = bf16[4,4,16,512]{3,2,1,0:T(8,128)(2,1)} copy(bf16[4,4,16,512]{3,2,1,0:T(8,128)(2,1)S(1)} %copy-done) | data formatting | bytes 524288
Async XLA Ops:
  66.2 2.7 %copy-start = (bf16[4,4,16,512]{3,2,1,0:T(8,128)(2,1)S(1)}, bf16[4,4,16,512]{3,2,1,0:T(8,128)(2,1)}, u32[]{:S(2)}) copy-start(bf16[4,4,16,512]{3,2,1,0:T(8,128)(2,1)} %get-tuple-element.9) | copy-start | bytes 786436

commit v2 on v1

--- a/solution.py
+++ b/solution.py
@@ -47,7 +47,7 @@
     st, st_col, st_z, snd, rcv, own, fin,
     gsum, g_col, gz_src, g_z, lg_src, lg,
     l_sem, h_ss, h_rs, u_ss, u_rs, t_ss, t_rs, sc_ss, sc_rs, sz_ss, sz_rs,
-    r_ss, r_rs, a_ss, a_rs, gc_ss, gc_rs, gz_ss, gz_rs, lg_ss, lg_rs, e_ss, e_rs,
+    r_ss, r_rs, a_ss, a_rs, gc_ss, gc_rs, gz_ss, gz_rs, lg_ss, lg_rs, e_ss, e_rs, z_sem,
 ):
     d, s, k = lax.axis_index("dp"), lax.axis_index("spatial"), lax.axis_index("code")
     z, yh, c = k // 4, (k // 2) % 2, k % 2
@@ -85,9 +85,8 @@
     load_x = pltpu.make_async_copy(feat, xp.at[:, pl.ds(1, BAND)], l_sem.at[2])
     load_w = pltpu.make_async_copy(cw_hbm, cw, l_sem.at[3])
     barrier = pltpu.get_barrier_semaphore()
-    peers = [xdev(o) for o in range(1, NX)] + [coldev(i) for i in range(1, 8)]
-    peers += [zdev(i) for i in range(1, NZ)] + [agdev(1, o) for o in range(1, NX)]
-    peers += [edgedev(e, i) for e in (1, NX - 1) for i in range(1, 4)]
+    peers = [xdev(1), xdev(NX - 1), ydev(1), ydev(NY - 1), zdev(1), zdev(NZ - 1)]
+    peers.append(dev(s, y, z, 1 - c))
     for who in peers:
         pl.semaphore_signal(barrier, inc=1, device_id=who, device_id_type=MESH)
     load_cb.start()
@@ -121,6 +120,12 @@
     for cp in halo + give_u:
         cp.start()
 
+    def tell(n, reach):
+        for i in (reach, NZ - reach):
+            pl.semaphore_signal(z_sem.at[n], inc=1, device_id=zdev(i), device_id_type=MESH)
+
+    tell(0, 1)
+
     def project(rb):
         u = right[rb * ROWS:(rb + 1) * ROWS, :]
 
@@ -157,6 +162,10 @@
     lat_hi = latent.astype(BF)
     right[2 * ROWS:3 * ROWS, :] = lat_hi
     lat_lo[:ROWS, :] = (latent - lat_hi.astype(F32)).astype(BF)
+    pl.semaphore_wait(z_sem.at[0], 2)
+    tell(1, 2)
+    for cp in give_u:
+        cp.wait_recv()
     give_t = []
     for n in range(2):
         rows = pl.ds(2 * ROWS + n * hrows, hrows)
@@ -198,8 +207,7 @@
             st[4 + 2 * rb + n:5 + 2 * rb + n, :] = mean[:, n * 128:(n + 1) * 128]
 
     score(0)
-    for cp in give_u:
-        cp.wait_recv()
+    pl.semaphore_wait(z_sem.at[1], 2)
     project(1)
     for cp in give_t:
         cp.wait_recv()
@@ -341,6 +349,51 @@
     keep.wait()
     for cp in out:
         cp.wait()
+
+
+def finish_kernel(factor, cg, fg, out_cg, out_fg, got, wide, fgv, i_sem, o_sem):
+    parts = got.shape[0]
+    rows = CODES // parts
+    take_fg = pltpu.make_async_copy(fg, fgv, i_sem.at[parts])
+    takes, gives = [], []
+    for n in range(parts):
+        at = pl.ds(n * rows, rows)
+        takes.append(pltpu.make_async_copy(cg.at[at], got.at[n], i_sem.at[n]))
+        gives.append(pltpu.make_async_copy(wide.at[n], out_cg.at[at], o_sem.at[n]))
+    gives.append(pltpu.make_async_copy(fgv, out_fg, o_sem.at[parts]))
+    for cp in takes + [take_fg]:
+        cp.start()
+    for n in range(parts):
+        takes[n].wait()
+        wide[n] = got[n].astype(F32) * factor
+        gives[n].start()
+    take_fg.wait()
+    gives[parts].start()
+    for cp in gives:
+        cp.wait()
+
+
+def finish(cg, fg, factor):
+    parts = 8
+    hbm = pl.BlockSpec(memory_space=pl.ANY)
+    return pl.pallas_call(
+        functools.partial(finish_kernel, factor),
+        out_shape=(
+            jax.ShapeDtypeStruct(cg.shape, F32),
+            jax.ShapeDtypeStruct(fg.shape, BF),
+        ),
+        in_specs=[hbm, hbm],
+        out_specs=(hbm, hbm),
+        scratch_shapes=[
+            pltpu.VMEM((parts, CODES // parts, HD), BF),
+            pltpu.VMEM((parts, CODES // parts, HD), F32),
+            pltpu.VMEM(fg.shape, BF),
+            pltpu.SemaphoreType.DMA((parts + 1,)),
+            pltpu.SemaphoreType.DMA((parts + 1,)),
+        ],
+        compiler_params=pltpu.CompilerParams(vmem_limit_bytes=56 << 20),
+        name="widen",
+    )(cg, fg)
 
 
 def on_device(features, conv_weight, codebook, recon_grad):
@@ -382,7 +435,7 @@
             vm((NZ - 1, OWN, D), BF),
             vm((BAND, LW, D), BF),
             vm((IMG, BAND + 2, LW, D), BF),
-        ] + [dma((n,)) for n in sems],
+        ] + [dma((n,)) for n in sems] + [pltpu.SemaphoreType.REGULAR((2,))],
         compiler_params=pltpu.CompilerParams(
             collective_id=0, has_side_effects=True, vmem_limit_bytes=56 << 20
         ),
@@ -393,7 +446,7 @@
     )(features, conv_weight, codebook, recon_grad.reshape(ROWS, D))
     entries_all = codebook.shape[0] * lax.axis_size("code")
     rows_all = ROWS * lax.axis_size("dp") * lax.axis_size("spatial")
-    return cg.astype(F32) * (entries_all / rows_all), fg
+    return finish(cg, fg, entries_all / rows_all)
 
 
 def solution(mesh):

time: 69.8 us -> 67.6 us (0.968)
  other arithmetic: 2.72 us -> 0 us
  Pallas kernels: 65.6 us -> 66.8 us
  local copies, waits for them, and re-layouts: 0.71 us -> 0 us
    mul x1 -> x0, other arithmetic: 2.72 us -> none  [on_device(): return (cg.astype(F32) * (entries_all / rows_all), fg)]
    pallas_call x0 -> x1, Pallas kernels: none -> 2.47 us  [finish(): pl.pallas_call(functools.partial(finish_kernel, factor), out_shape=(jax.S...]
    pallas_call x1, Pallas kernels: 65.6 us -> 64.3 us  [on_device(): pl.pallas_call(kernel, out_shape=(jax.ShapeDtypeStruct((CODES, HD), BF),...]
    unnamed x3 -> x0, local copies, waits for them, and re-layouts: 0.71 us -> none
where the time goes in v2:
time: 67.6 us; the launch traced here: 67.5 us
  Pallas kernels  66.8 us (99%)
    pallas_call x1, Pallas kernels, on_device(): pl.pallas_call(kernel, out_shape=(jax.ShapeDtypeStruct((CODES, HD), BF),...  64.3 us
    pallas_call x1, Pallas kernels, finish(): pl.pallas_call(functools.partial(finish_kernel, factor), out_shape=(jax.S...  2.47 us

profile of v2, /device:TPU:1, one launch (start us, length us, event | category | flops | bytes accessed | tf_op | source)
XLA Modules:
  0.0 67.5 jit_solution(17779331665363381791)
XLA Ops:
  0.6 64.3 %soft_quantize.1 = (bf16[4096,128]{1,0:T(8,128)(2,1)}, bf16[4,4,16,512]{3,2,1,0:T(8,128)(2,1)}) custom-call(bf16[4,4,16,512]{3,2,1,0:T(8,128)(2,1)} %feat.1, bf16[3,3,512,256]{3,2,1,0:T(8,128)(2,1)} %cw_hbm.1, f32[4096,256]{1,0:T(8,128)} %cb_hbm.1, bf16[256,256]{1,0:T(8,128)(2,1)} %bitcast.1), custom_call_target="tpu_custom_call" | custom-call | flops 12884901888 | bytes 10485760 | tf_op jit(solution)/shard_map/soft_quantize/pallas_call | solution.py:404
  65.0 2.5 %widen.1 = (f32[4096,128]{1,0:T(8,128)}, bf16[4,4,16,512]{3,2,1,0:T(8,128)(2,1)}) custom-call(bf16[4096,128]{1,0:T(8,128)(2,1)} %get-tuple-element.4.cg, bf16[4,4,16,512]{3,2,1,0:T(8,128)(2,1)} %get-tuple-element.5.fg), custom_call_target="tpu_custom_call" | custom-call | tf_op jit(solution)/shard_map/widen/pallas_call | solution.py:379

commit v3 on v2

--- a/solution.py
+++ b/solution.py
@@ -16,9 +16,10 @@
 CODES = 4096
 HALF = CODES // 2
 BLK = HALF // NX
+PART = BLK // 2
+QTR = PART // 2
 OWN = IMG * BAND * LW // 4
 HD = D // 2
-EDGE_SEMS = 8
 
 
 def nt(a, b):
@@ -44,10 +45,10 @@
     feat, cw_hbm, cb_hbm, up,
     cg, fg,
     xp, cw, cb, hi, lo, right, lat_lo, wts, proj, mst, pg, gb,
-    st, st_col, st_z, snd, rcv, own, fin,
-    gsum, g_col, gz_src, g_z, lg_src, lg,
+    st, st_col, st_z, far, near, mid, got_far, got_left, got_right, own, fin,
+    hi_t, gsum, g_col, gz_src, g_z, lg_src, lg,
     l_sem, h_ss, h_rs, u_ss, u_rs, t_ss, t_rs, sc_ss, sc_rs, sz_ss, sz_rs,
-    r_ss, r_rs, a_ss, a_rs, gc_ss, gc_rs, gz_ss, gz_rs, lg_ss, lg_rs, e_ss, e_rs, z_sem,
+    r2_ss, r2_rs, rd_ss, rd_rs, rm_ss, rm_rs, a_ss, a_rs, gc_ss, gc_rs, gz_ss, gz_rs, lg_ss, lg_rs, e_ss, e_rs, z_sem,
 ):
     d, s, k = lax.axis_index("dp"), lax.axis_index("spatial"), lax.axis_index("code")
     z, yh, c = k // 4, (k // 2) % 2, k % 2
@@ -137,6 +138,12 @@
     load_u.wait()
     project(0)
 
+    @pl.loop(0, HALF // 256)
+    def _(i):
+        at = pl.ds(pl.multiple_of(i * 256, 256), 256)
+        hi_t[:, at] = hi[at, :].T
+
+
     load_x.wait()
     load_w.wait()
     for cp in halo:
@@ -245,25 +252,41 @@
     inner = jnp.concatenate([mean[n:n + 1] for n in range(4)], axis=1)
 
     both = 2 * ROWS
-    sums = []
-    for o in (2, 1, 3, 0):
+
+    def term(o, h):
         blk = (s + o) % NX
-        rows = pl.ds(pl.multiple_of(blk * BLK, BLK), BLK)
+        rows = pl.ds(pl.multiple_of(blk * BLK + h * PART, PART), PART)
         p = wts[rows, :] * jnp.exp(mst[blk] - total)
         g = (p * (proj[rows, :] - inner)).astype(BF)
         pg[:, :both] = p.astype(BF)
         pg[:, both:] = g
         gb[rows, :] = g
-        term = nn(pg[...], right[...])
-        if o:
-            snd[o - 1] = term.astype(BF)
-            cp = remote(snd.at[o - 1], rcv.at[o - 1], r_ss.at[o - 1], r_rs.at[o - 1], xdev(o))
+        return nn(pg[...], right[...])
+
+    near_x = (1, NX - 1)
+    first, second = slice(0, QTR), slice(QTR, PART)
+    ring, direct, summed = [], [], []
+    for h in range(2):
+        t = term(2, h).astype(BF)
+        for n, half in enumerate((first, second)):
+            m = 2 * h + n
+            far[m] = t[half]
+            cp = remote(far.at[m], got_far.at[m], r2_ss.at[m], r2_rs.at[m], xdev(near_x[n]))
             cp.start()
-            sums.append(cp)
-        else:
-            own[...] = term
-
-    gsum[...] = tn(gb[...], hi[...]).astype(BF)
+            ring.append(cp)
+        for n, (now, later) in enumerate(((second, first), (first, second))):
+            m = 2 * h + n
+            t = term(near_x[n], h)
+            mid[m] = t[later]
+            near[m, now] = t[now].astype(BF)
+            at = pl.ds(now.start, QTR)
+            to = (got_left, got_right)[n]
+            cp = remote(near.at[m, at], to.at[h, at], rd_ss.at[m], rd_rs.at[m], xdev(near_x[n]))
+            cp.start()
+            direct.append(cp)
+    for h in range(2):
+        own[h] = term(0, h)
+    gsum[...] = nn(hi_t[...], gb[...]).T.astype(BF)
 
     def image(y_, c_):
         return (y_ // 2) * 2 + c_
@@ -276,6 +299,39 @@
         gcol.append(remote(gsum.at[rows], g_col.at[i - 1], gc_ss.at[i - 1], gc_rs.at[i - 1], coldev(i)))
     for cp in gcol:
         cp.start()
+
+    for h in range(2):
+        for n, later in enumerate((first, second)):
+            m = 2 * h + n
+            ring[m].wait_recv()
+            near[m, later] = (mid[m] + got_far[m].astype(F32)).astype(BF)
+            at = pl.ds(later.start, QTR)
+            to = (got_left, got_right)[n]
+            cp = remote(near.at[m, at], to.at[h, at], rm_ss.at[m], rm_rs.at[m], xdev(near_x[n]))
+            cp.start()
+            summed.append(cp)
+
+    out, keep = [], []
+
+    def spread(h):
+        for n in range(2):
+            direct[2 * h + n].wait_recv()
+            summed[2 * h + n].wait_recv()
+        block = own[h] + got_left[h].astype(F32) + got_right[h].astype(F32)
+        left, rest = block[:, :HD].astype(BF), block[:, HD:].astype(BF)
+        fin[h, 0] = jnp.where(d == 0, left, rest)
+        fin[h, 1] = jnp.where(d == 0, rest, left)
+        place = cg.at[pl.ds(pl.multiple_of(d * HALF + s * BLK + h * PART, PART), PART)]
+        for f in (0, 1):
+            for o in (2, 1, 3, 0):
+                if f or o:
+                    n = h * 8 + f * NX + o
+                    out.append(remote(fin.at[h, f], place, a_ss.at[n], a_rs.at[n], agdev(f, o)))
+                    out[-1].start()
+        keep.append(pltpu.make_async_copy(fin.at[h, 0], place, l_sem.at[4 + h]))
+        keep[-1].start()
+
+    spread(0)
     for cp in gcol:
         cp.wait_recv()
     img = image(y, c)
@@ -286,26 +342,7 @@
     gzs = [remote(gz_src, g_z.at[i - 1], gz_ss.at[i - 1], gz_rs.at[i - 1], zdev(i)) for i in range(1, NZ)]
     for cp in gzs:
         cp.start()
-
-    for cp in sums:
-        cp.wait_recv()
-    block = own[...]
-    for o in range(3):
-        block = block + rcv[o].astype(F32)
-    left, rest = block[:, :HD].astype(BF), block[:, HD:].astype(BF)
-    fin[0] = jnp.where(d == 0, left, rest)
-    fin[1] = jnp.where(d == 0, rest, left)
-    place = cg.at[pl.ds(pl.multiple_of(d * HALF + s * BLK, BLK), BLK)]
-    out = []
-    for f in (0, 1):
-        for o in (2, 1, 3, 0):
-            if f or o:
-                n = f * NX + o
-                out.append(remote(fin.at[f], place, a_ss.at[n], a_rs.at[n], agdev(f, o)))
-    for cp in out:
-        cp.start()
-    keep = pltpu.make_async_copy(fin.at[0], place, l_sem.at[4])
-    keep.start()
+    spread(1)
 
     for cp in gzs:
         cp.wait_recv()
@@ -344,10 +381,9 @@
     grad = back_taps(1) + shifted(back_taps(0), -1) + shifted(back_taps(2), 1)
     fg[...] = grad.astype(BF).reshape(IMG, BAND, LW, CIN)
 
-    for cp in halo + give_u + give_t + col + zs + sums + gcol + gzs + back:
+    for cp in halo + give_u + give_t + col + zs + ring + direct + summed + gcol + gzs + back:
         cp.wait_send()
-    keep.wait()
-    for cp in out:
+    for cp in keep + out:
         cp.wait()
 
 
@@ -400,7 +436,7 @@
     dma = pltpu.SemaphoreType.DMA
     vm = pltpu.VMEM
     hbm = pl.BlockSpec(memory_space=pl.ANY)
-    sems = [5, 2, 2, 2, 2, 4, 4, 7, 7, 7, 7, 3, 3, 8, 8, 7, 7, 7, 7, 3, 3, 8, 8]
+    sems = [6, 2, 2, 2, 2, 4, 4, 7, 7, 7, 7, 4, 4, 4, 4, 4, 4, 16, 16, 7, 7, 7, 7, 3, 3, 8, 8]
     cg, fg = pl.pallas_call(
         kernel,
         out_shape=(
@@ -420,15 +456,20 @@
             vm((HALF, 2 * ROWS), F32),
             vm((HALF, 2 * ROWS), F32),
             vm((NX, 1, 2 * ROWS), F32),
-            vm((BLK, 4 * ROWS), BF),
+            vm((PART, 4 * ROWS), BF),
             vm((HALF, 2 * ROWS), BF),
             vm((8, 128), F32),
             vm((7, 8, 128), F32),
             vm((NZ, 8, 128), F32),
-            vm((3, BLK, D), BF),
-            vm((3, BLK, D), BF),
-            vm((BLK, D), F32),
-            vm((2, BLK, HD), BF),
+            vm((4, QTR, D), BF),
+            vm((4, PART, D), BF),
+            vm((4, QTR, D), F32),
+            vm((4, QTR, D), BF),
+            vm((2, PART, D), BF),
+            vm((2, PART, D), BF),
+            vm((2, PART, D), F32),
+            vm((2, 2, PART, HD), BF),
+            vm((D, HALF), BF),
             vm((2 * ROWS, D), BF),
             vm((7, OWN, D), BF),
             vm((OWN, D), BF),

time: 67.6 us -> 61 us (0.902)
  Pallas kernels: 66.8 us -> 60.2 us
    pallas_call x1, Pallas kernels: 64.3 us -> 57.7 us  [on_device(): pl.pallas_call(kernel, out_shape=(jax.ShapeDtypeStruct((CODES, HD), BF),...]
where the time goes in v3:
time: 61 us; the launch traced here: 60.8 us
  Pallas kernels  60.2 us (99%)
  between operations  0.64 us (1%)
    pallas_call x1, Pallas kernels, on_device(): pl.pallas_call(kernel, out_shape=(jax.ShapeDtypeStruct((CODES, HD), BF),...  57.7 us
    pallas_call x1, Pallas kernels, finish(): pl.pallas_call(functools.partial(finish_kernel, factor), out_shape=(jax.S...  2.47 us

profile of v3, /device:TPU:1, one launch (start us, length us, event | category | flops | bytes accessed | tf_op | source)
XLA Modules:
  0.0 60.8 jit_solution(10314371828047714584)
XLA Ops:
  0.6 57.7 %soft_quantize.1 = (bf16[4096,128]{1,0:T(8,128)(2,1)}, bf16[4,4,16,512]{3,2,1,0:T(8,128)(2,1)}) custom-call(bf16[4,4,16,512]{3,2,1,0:T(8,128)(2,1)} %feat.1, bf16[3,3,512,256]{3,2,1,0:T(8,128)(2,1)} %cw_hbm.1, f32[4096,256]{1,0:T(8,128)} %cb_hbm.1, bf16[256,256]{1,0:T(8,128)(2,1)} %bitcast.1), custom_call_target="tpu_custom_call" | custom-call | flops 12884901888 | bytes 10485760 | tf_op jit(solution)/shard_map/soft_quantize/pallas_call | solution.py:440
  58.4 2.5 %widen.1 = (f32[4096,128]{1,0:T(8,128)}, bf16[4,4,16,512]{3,2,1,0:T(8,128)(2,1)}) custom-call(bf16[4096,128]{1,0:T(8,128)(2,1)} %get-tuple-element.4.cg, bf16[4,4,16,512]{3,2,1,0:T(8,128)(2,1)} %get-tuple-element.5.fg), custom_call_target="tpu_custom_call" | custom-call | tf_op jit(solution)/shard_map/widen/pallas_call | solution.py:415

commit v4 on v3

--- a/solution.py
+++ b/solution.py
@@ -18,7 +18,8 @@
 BLK = HALF // NX
 PART = BLK // 2
 QTR = PART // 2
-OWN = IMG * BAND * LW // 4
+OWN = IMG * LW
+UNIT = OWN // LW
 HD = D // 2
 
 
@@ -44,7 +45,7 @@
 def kernel(
     feat, cw_hbm, cb_hbm, up,
     cg, fg,
-    xp, cw, cb, hi, lo, right, lat_lo, wts, proj, mst, pg, gb,
+    xp, cw, cb, hi, lo, right, lat_lo, wts, proj, mst, pg, wb, gb, sum_w, sum_g,
     st, st_col, st_z, far, near, mid, got_far, got_left, got_right, own, fin,
     hi_t, gsum, g_col, gz_src, g_z, lg_src, lg,
     l_sem, h_ss, h_rs, u_ss, u_rs, t_ss, t_rs, sc_ss, sc_rs, sz_ss, sz_rs,
@@ -82,18 +83,22 @@
         )
 
     load_cb = pltpu.make_async_copy(cb_hbm.at[pl.ds(d * HALF, HALF)], cb, l_sem.at[0])
-    load_u = pltpu.make_async_copy(up, right.at[pl.ds(0, ROWS)], l_sem.at[1])
-    load_x = pltpu.make_async_copy(feat, xp.at[:, pl.ds(1, BAND)], l_sem.at[2])
-    load_w = pltpu.make_async_copy(cw_hbm, cw, l_sem.at[3])
+    load_u = [
+        pltpu.make_async_copy(up.at[:, h], right.at[pl.ds(h * UNIT, UNIT)], l_sem.at[4 + h])
+        for h in range(BAND)
+    ]
+    load_x = [
+        pltpu.make_async_copy(feat.at[:, h], xp.at[1 + h], l_sem.at[8 + h]) for h in range(BAND)
+    ]
+    load_w = pltpu.make_async_copy(cw_hbm, cw, l_sem.at[1])
     barrier = pltpu.get_barrier_semaphore()
     peers = [xdev(1), xdev(NX - 1), ydev(1), ydev(NY - 1), zdev(1), zdev(NZ - 1)]
     peers.append(dev(s, y, z, 1 - c))
     for who in peers:
         pl.semaphore_signal(barrier, inc=1, device_id=who, device_id_type=MESH)
     load_cb.start()
-    load_u.start()
-    load_x.start()
-    load_w.start()
+    for cp in load_x + [load_w] + load_u:
+        cp.start()
     load_cb.wait()
 
     @pl.loop(0, HALF // 256)
@@ -106,17 +111,22 @@
 
     pl.semaphore_wait(barrier, len(peers))
 
+    for cp in load_u:
+        cp.wait()
     halo = [
-        remote(feat.at[:, BAND - 1], xp.at[:, 0], h_ss.at[0], h_rs.at[0], xdev(1)),
-        remote(feat.at[:, 0], xp.at[:, BAND + 1], h_ss.at[1], h_rs.at[1], xdev(NX - 1)),
+        remote(feat.at[:, BAND - 1], xp.at[0], h_ss.at[0], h_rs.at[0], xdev(1)),
+        remote(feat.at[:, 0], xp.at[BAND + 1], h_ss.at[1], h_rs.at[1], xdev(NX - 1)),
     ]
-    hrows = ROWS // 2
+    sides = (1, NY - 1)
+
+    def share(buf, at, count, peer_at, ss, rs, n):
+        return remote(
+            buf.at[pl.ds(at, count)], buf.at[pl.ds(peer_at, count)], ss.at[n], rs.at[n], ydev(sides[n % 2])
+        )
+
+    quarter = ROWS // LW
     give_u = [
-        remote(
-            up.at[pl.ds(n * hrows, hrows)], right.at[pl.ds(ROWS + n * hrows, hrows)],
-            u_ss.at[n], u_rs.at[n], ydev((1, 3)[n]),
-        )
-        for n in range(2)
+        share(right, n * 2 * UNIT, 2 * UNIT, quarter + n * 2 * UNIT, u_ss, u_rs, n) for n in range(2)
     ]
     for cp in halo + give_u:
         cp.start()
@@ -127,15 +137,45 @@
 
     tell(0, 1)
 
+    def rows_of(buf, n):
+        return buf[n * quarter:(n + 1) * quarter].reshape(ROWS, D)
+
     def project(rb):
-        u = right[rb * ROWS:(rb + 1) * ROWS, :]
-
-        @pl.loop(0, NX)
-        def _(i):
-            rows = pl.ds(pl.multiple_of(i * BLK, BLK), BLK)
+        u = rows_of(right, rb)
+        for i in range(NX):
+            rows = slice(i * BLK, (i + 1) * BLK)
             proj[rows, rb * ROWS:(rb + 1) * ROWS] = nt(hi[rows, :], u) + nt(lo[rows, :], u)
 
-    load_u.wait()
+    give_t = []
+
+    def convolve(grid_rows):
+        def taps(b):
+            acc = None
+            for a in range(3):
+                xa = jnp.concatenate([xp[h + a].reshape(OWN, CIN) for h in grid_rows], axis=0)
+                t = nn(xa, cw[a, b])
+                acc = t if acc is None else acc + t
+            return acc
+
+        latent = taps(1) + shifted(taps(0), 1) + shifted(taps(2), -1)
+        lat_hi = latent.astype(BF)
+        rest = (latent - lat_hi.astype(F32)).astype(BF)
+        for n, h in enumerate(grid_rows):
+            at = slice(n * OWN, (n + 1) * OWN)
+            right[2 * quarter + h * UNIT:2 * quarter + (h + 1) * UNIT] = lat_hi[at].reshape(UNIT, LW, D)
+            lat_lo[h * UNIT:(h + 1) * UNIT] = rest[at].reshape(UNIT, LW, D)
+        for n, h in enumerate(grid_rows):
+            m = len(give_t)
+            give_t.append(share(right, 2 * quarter + h * UNIT, UNIT, 3 * quarter + h * UNIT, t_ss, t_rs, m))
+            give_t[-1].start()
+        for n, h in enumerate(grid_rows):
+            m = len(give_t)
+            give_t.append(share(lat_lo, h * UNIT, UNIT, quarter + h * UNIT, t_ss, t_rs, m))
+            give_t[-1].start()
+
+    for cp in load_x + [load_w]:
+        cp.wait()
+    convolve((1, 2))
     project(0)
 
     @pl.loop(0, HALF // 256)
@@ -143,46 +183,20 @@
         at = pl.ds(pl.multiple_of(i * 256, 256), 256)
         hi_t[:, at] = hi[at, :].T
 
-
-    load_x.wait()
-    load_w.wait()
-    for cp in halo:
+    pl.semaphore_wait(z_sem.at[0], 2)
+    tell(1, 2)
+    for cp in halo + give_u:
         cp.wait_recv()
 
     @pl.when(s == 0)
     def _():
-        xp[:, 0] = jnp.zeros((IMG, LW, CIN), BF)
+        xp[0] = jnp.zeros((IMG, LW, CIN), BF)
 
     @pl.when(s == NX - 1)
     def _():
-        xp[:, BAND + 1] = jnp.zeros((IMG, LW, CIN), BF)
-
-    def taps(b):
-        acc = None
-        for a in range(3):
-            xa = xp[:, a:a + BAND].reshape(ROWS, CIN)
-            t = nn(xa, cw[a, b])
-            acc = t if acc is None else acc + t
-        return acc
-
-    latent = taps(1) + shifted(taps(0), 1) + shifted(taps(2), -1)
-    lat_hi = latent.astype(BF)
-    right[2 * ROWS:3 * ROWS, :] = lat_hi
-    lat_lo[:ROWS, :] = (latent - lat_hi.astype(F32)).astype(BF)
-    pl.semaphore_wait(z_sem.at[0], 2)
-    tell(1, 2)
-    for cp in give_u:
-        cp.wait_recv()
-    give_t = []
-    for n in range(2):
-        rows = pl.ds(2 * ROWS + n * hrows, hrows)
-        to = pl.ds(3 * ROWS + n * hrows, hrows)
-        give_t.append(remote(right.at[rows], right.at[to], t_ss.at[n], t_rs.at[n], ydev((1, 3)[n])))
-        rows = pl.ds(n * hrows, hrows)
-        to = pl.ds(ROWS + n * hrows, hrows)
-        give_t.append(remote(lat_lo.at[rows], lat_lo.at[to], t_ss.at[2 + n], t_rs.at[2 + n], ydev((1, 3)[n])))
-    for cp in give_t:
-        cp.start()
+        xp[BAND + 1] = jnp.zeros((IMG, LW, CIN), BF)
+
+    convolve((0, BAND - 1))
 
     def merge(a, b):
         top = jnp.maximum(a[0], b[0])
@@ -191,11 +205,11 @@
 
     def score(rb):
         cols = slice(rb * ROWS, (rb + 1) * ROWS)
-        lh = right[(2 + rb) * ROWS:(3 + rb) * ROWS, :]
-        ll = lat_lo[cols, :]
+        lh = rows_of(right, 2 + rb)
+        ll = rows_of(lat_lo, rb)
 
         def step(i, carry):
-            rows = pl.ds(pl.multiple_of(i * BLK, BLK), BLK)
+            rows = slice(i * BLK, (i + 1) * BLK)
             h = hi[rows, :]
             sc = nt(h, lh) + (nt(h, ll) + nt(lo[rows, :], lh))
             top = jnp.max(sc, axis=0, keepdims=True)
@@ -207,18 +221,22 @@
             return merge(carry, (top, mass, dots))
 
         zero = jnp.zeros((1, ROWS), F32)
-        top, mass, dots = lax.fori_loop(0, NX, step, (zero - 3.0e38, zero, zero))
+        carry = (zero - 3.0e38, zero, zero)
+        for i in range(NX):
+            carry = step(i, carry)
+        top, mass, dots = carry
         logs, mean = top + jnp.log(mass), dots / mass
         for n in range(2):
             st[2 * rb + n:2 * rb + n + 1, :] = logs[:, n * 128:(n + 1) * 128]
             st[4 + 2 * rb + n:5 + 2 * rb + n, :] = mean[:, n * 128:(n + 1) * 128]
-
-    score(0)
+        return logs, mean
+
+    ends = [score(0)]
     pl.semaphore_wait(z_sem.at[1], 2)
     project(1)
     for cp in give_t:
         cp.wait_recv()
-    score(1)
+    ends.append(score(1))
 
     def combine(parts):
         top = functools.reduce(jnp.maximum, [p[:4] for p in parts])
@@ -234,6 +252,17 @@
     col = [remote(st, st_col.at[i - 1], sc_ss.at[i - 1], sc_rs.at[i - 1], coldev(i)) for i in range(1, 8)]
     for cp in col:
         cp.start()
+
+    own_logs = jnp.concatenate([e[0] for e in ends], axis=1)
+    own_mean = jnp.concatenate([e[1] for e in ends], axis=1)
+    for i in range(2 * NX):
+        rows = slice(i * PART, (i + 1) * PART)
+        w = wts[rows, :] * jnp.exp(mst[i // 2] - own_logs)
+        wb[rows, :] = w.astype(BF)
+        gb[rows, :] = (w * (proj[rows, :] - own_mean)).astype(BF)
+    sum_g[...] = nn(hi_t[...], gb[...])
+    sum_w[...] = nn(hi_t[...], wb[...])
+
     for cp in col:
         cp.wait_recv()
     parts = [st[...]]
@@ -260,8 +289,20 @@
         g = (p * (proj[rows, :] - inner)).astype(BF)
         pg[:, :both] = p.astype(BF)
         pg[:, both:] = g
-        gb[rows, :] = g
-        return nn(pg[...], right[...])
+        return nn(pg[...], right[...].reshape(4 * ROWS, D))
+
+    share_of = jnp.exp(own_logs - total)
+    gsum[...] = (share_of * (sum_g[...] + (own_mean - inner) * sum_w[...])).T.astype(BF)
+
+    def grid_row(y_, c_):
+        return (y_ // 2) * 2 + c_
+
+    gcol = []
+    for i in range(1, 8):
+        j = i // 2
+        base = (j % 2) * ROWS + grid_row((y + j) % NY, (c + i) % 2) * OWN
+        rows = pl.ds(pl.multiple_of(base, OWN), OWN)
+        gcol.append(remote(gsum.at[rows], g_col.at[i - 1], gc_ss.at[i - 1], gc_rs.at[i - 1], coldev(i)))
 
     near_x = (1, NX - 1)
     first, second = slice(0, QTR), slice(QTR, PART)
@@ -284,22 +325,10 @@
             cp = remote(near.at[m, at], to.at[h, at], rd_ss.at[m], rd_rs.at[m], xdev(near_x[n]))
             cp.start()
             direct.append(cp)
+    for cp in gcol:
+        cp.start()
     for h in range(2):
         own[h] = term(0, h)
-    gsum[...] = nn(hi_t[...], gb[...]).T.astype(BF)
-
-    def image(y_, c_):
-        return (y_ // 2) * 2 + c_
-
-    gcol = []
-    for i in range(1, 8):
-        j = i // 2
-        base = (j % 2) * ROWS + image((y + j) % NY, (c + i) % 2) * OWN
-        rows = pl.ds(pl.multiple_of(base, OWN), OWN)
-        gcol.append(remote(gsum.at[rows], g_col.at[i - 1], gc_ss.at[i - 1], gc_rs.at[i - 1], coldev(i)))
-    for cp in gcol:
-        cp.start()
-
     for h in range(2):
         for n, later in enumerate((first, second)):
             m = 2 * h + n
@@ -328,14 +357,14 @@
                     n = h * 8 + f * NX + o
                     out.append(remote(fin.at[h, f], place, a_ss.at[n], a_rs.at[n], agdev(f, o)))
                     out[-1].start()
-        keep.append(pltpu.make_async_copy(fin.at[h, 0], place, l_sem.at[4 + h]))
+        keep.append(pltpu.make_async_copy(fin.at[h, 0], place, l_sem.at[2 + h]))
         keep[-1].start()
 
     spread(0)
     for cp in gcol:
         cp.wait_recv()
-    img = image(y, c)
-    part = gsum[pl.ds(pl.multiple_of(img * OWN, OWN), OWN), :].astype(F32)
+    mine = grid_row(y, c)
+    part = gsum[pl.ds(pl.multiple_of(mine * OWN, OWN), OWN), :].astype(F32)
     for i in range(7):
         part = part + g_col[i].astype(F32)
     gz_src[...] = part.astype(BF)
@@ -348,38 +377,55 @@
         cp.wait_recv()
     for i in range(NZ - 1):
         part = part + g_z[i].astype(F32)
-    lg_src[...] = part.astype(BF).reshape(BAND, LW, D)
-    lg[img, pl.ds(1, BAND)] = lg_src[...]
-    back = []
-    for n, i in enumerate((1, 4, 5)):
-        back.append(remote(lg_src, lg.at[img, pl.ds(1, BAND)], lg_ss.at[n], lg_rs.at[n], coldev(i)))
-    for n, (e, edge, to) in enumerate(((1, BAND - 1, 0), (NX - 1, 0, BAND + 1))):
-        for i in range(4):
-            m = n * 4 + i
-            back.append(remote(lg_src.at[edge], lg.at[img, to], e_ss.at[m], e_rs.at[m], edgedev(e, i)))
+    lg_src[...] = part.astype(BF)
+    lg[1 + mine] = lg_src[...]
+    back = [
+        remote(lg_src, lg.at[1 + mine], lg_ss.at[n], lg_rs.at[n], coldev(i))
+        for n, i in enumerate((1, 4, 5))
+    ]
+    edges = []
+    for n, (e, to) in enumerate(((1, 0), (NX - 1, BAND + 1))):
+        edges.append([
+            remote(lg_src, lg.at[to], e_ss.at[n * 4 + i], e_rs.at[n], edgedev(e, i)) for i in range(4)
+        ])
+    edge_row = (BAND - 1, 0)
+    for n in range(2):
+
+        @pl.when(mine == edge_row[n])
+        def _():
+            for cp in edges[n]:
+                cp.start()
+
     for cp in back:
         cp.start()
-    for cp in back:
+    for cp in back + [edges[0][0], edges[1][0]]:
         cp.wait_recv()
 
     @pl.when(s == 0)
     def _():
-        lg[:, 0] = jnp.zeros((IMG, LW, D), BF)
+        lg[0] = jnp.zeros((OWN, D), BF)
 
     @pl.when(s == NX - 1)
     def _():
-        lg[:, BAND + 1] = jnp.zeros((IMG, LW, D), BF)
+        lg[BAND + 1] = jnp.zeros((OWN, D), BF)
 
     def back_taps(b):
         acc = None
         for a in range(3):
-            la = lg[:, 2 - a:2 - a + BAND].reshape(ROWS, D)
+            la = lg[2 - a:2 - a + BAND].reshape(ROWS, D)
             t = nt(la, cw[a, b])
             acc = t if acc is None else acc + t
         return acc
 
     grad = back_taps(1) + shifted(back_taps(0), -1) + shifted(back_taps(2), 1)
-    fg[...] = grad.astype(BF).reshape(IMG, BAND, LW, CIN)
+    for h in range(BAND):
+        fg[:, h] = grad[h * OWN:(h + 1) * OWN].astype(BF).reshape(IMG, LW, CIN)
+    for n in range(2):
+
+        @pl.when(mine == edge_row[n])
+        def _():
+            for cp in edges[n]:
+                cp.wait_send()
 
     for cp in halo + give_u + give_t + col + zs + ring + direct + summed + gcol + gzs + back:
         cp.wait_send()
@@ -436,7 +482,7 @@
     dma = pltpu.SemaphoreType.DMA
     vm = pltpu.VMEM
     hbm = pl.BlockSpec(memory_space=pl.ANY)
-    sems = [6, 2, 2, 2, 2, 4, 4, 7, 7, 7, 7, 4, 4, 4, 4, 4, 4, 16, 16, 7, 7, 7, 7, 3, 3, 8, 8]
+    sems = [12, 2, 2, 2, 2, 8, 8, 7, 7, 7, 7, 4, 4, 4, 4, 4, 4, 16, 16, 7, 7, 7, 7, 3, 3, 8, 2]
     cg, fg = pl.pallas_call(
         kernel,
         out_shape=(
@@ -446,18 +492,21 @@
         in_specs=[hbm] * 4,
         out_specs=(hbm, pl.BlockSpec(memory_space=pltpu.VMEM)),
         scratch_shapes=[
-            vm((IMG, BAND + 2, LW, CIN), BF),
+            vm((BAND + 2, IMG, LW, CIN), BF),
             vm((3, 3, CIN, D), BF),
             vm((HALF, D), F32),
             vm((HALF, D), BF),
             vm((HALF, D), BF),
-            vm((4 * ROWS, D), BF),
-            vm((2 * ROWS, D), BF),
+            vm((4 * ROWS // LW, LW, D), BF),
+            vm((2 * ROWS // LW, LW, D), BF),
             vm((HALF, 2 * ROWS), F32),
             vm((HALF, 2 * ROWS), F32),
             vm((NX, 1, 2 * ROWS), F32),
             vm((PART, 4 * ROWS), BF),
             vm((HALF, 2 * ROWS), BF),
+            vm((HALF, 2 * ROWS), BF),
+            vm((D, 2 * ROWS), F32),
+            vm((D, 2 * ROWS), F32),
             vm((8, 128), F32),
             vm((7, 8, 128), F32),
             vm((NZ, 8, 128), F32),
@@ -474,8 +523,8 @@
             vm((7, OWN, D), BF),
             vm((OWN, D), BF),
             vm((NZ - 1, OWN, D), BF),
-            vm((BAND, LW, D), BF),
-            vm((IMG, BAND + 2, LW, D), BF),
+            vm((OWN, D), BF),
+            vm((BAND + 2, OWN, D), BF),
         ] + [dma((n,)) for n in sems] + [pltpu.SemaphoreType.REGULAR((2,))],
         compiler_params=pltpu.CompilerParams(
             collective_id=0, has_side_effects=True, vmem_limit_bytes=56 << 20
@@ -484,7 +533,7 @@
             flops=12 * 2**30, bytes_accessed=10 << 20, transcendentals=1 << 21
         ),
         name="soft_quantize",
-    )(features, conv_weight, codebook, recon_grad.reshape(ROWS, D))
+    )(features, conv_weight, codebook, recon_grad)
     entries_all = codebook.shape[0] * lax.axis_size("code")
     rows_all = ROWS * lax.axis_size("dp") * lax.axis_size("spatial")
     return finish(cg, fg, entries_all / rows_all)

time: 61 us -> 59.8 us (0.980)
  Pallas kernels: 60.2 us -> 59.1 us
    pallas_call x1, Pallas kernels: 57.7 us -> 56.6 us  [on_device(): pl.pallas_call(kernel, out_shape=(jax.ShapeDtypeStruct((CODES, HD), BF),...]
where the time goes in v4:
time: 59.8 us; the launch traced here: 59.7 us
  Pallas kernels  59.1 us (99%)
  between operations  0.64 us (1%)
    pallas_call x1, Pallas kernels, on_device(): pl.pallas_call(kernel, out_shape=(jax.ShapeDtypeStruct((CODES, HD), BF),...  56.6 us
    pallas_call x1, Pallas kernels, finish(): pl.pallas_call(functools.partial(finish_kernel, factor), out_shape=(jax.S...  2.47 us

profile of v4, /device:TPU:1, one launch (start us, length us, event | category | flops | bytes accessed | tf_op | source)
XLA Modules:
  0.0 59.7 jit_solution(1405018992572082164)
XLA Ops:
  0.6 56.6 %soft_quantize.1 = (bf16[4096,128]{1,0:T(8,128)(2,1)}, bf16[4,4,16,512]{3,2,1,0:T(8,128)(2,1)}) custom-call(bf16[4,4,16,512]{3,2,1,0:T(8,128)(2,1)} %feat.1, bf16[3,3,512,256]{3,2,1,0:T(8,128)(2,1)} %cw_hbm.1, f32[4096,256]{1,0:T(8,128)} %cb_hbm.1, bf16[4,4,16,256]{3,2,1,0:T(8,128)(2,1)} %up.1), custom_call_target="tpu_custom_call" | custom-call | flops 12884901888 | bytes 10485760 | tf_op jit(solution)/shard_map/soft_quantize/pallas_call | solution.py:486
  57.3 2.5 %widen.1 = (f32[4096,128]{1,0:T(8,128)}, bf16[4,4,16,512]{3,2,1,0:T(8,128)(2,1)}) custom-call(bf16[4096,128]{1,0:T(8,128)(2,1)} %get-tuple-element.4.cg, bf16[4,4,16,512]{3,2,1,0:T(8,128)(2,1)} %get-tuple-element.5.fg), custom_call_target="tpu_custom_call" | custom-call | tf_op jit(solution)/shard_map/widen/pallas_call | solution.py:461

commit v5 on v4

--- a/solution.py
+++ b/solution.py
@@ -340,6 +340,17 @@
             cp.start()
             summed.append(cp)
 
+    for cp in gcol:
+        cp.wait_recv()
+    mine = grid_row(y, c)
+    part = gsum[pl.ds(pl.multiple_of(mine * OWN, OWN), OWN), :].astype(F32)
+    for i in range(7):
+        part = part + g_col[i].astype(F32)
+    gz_src[...] = part.astype(BF)
+    gzs = [remote(gz_src, g_z.at[i - 1], gz_ss.at[i - 1], gz_rs.at[i - 1], zdev(i)) for i in range(1, NZ)]
+    for cp in gzs:
+        cp.start()
+
     out, keep = [], []
 
     def spread(h):
@@ -361,17 +372,6 @@
         keep[-1].start()
 
     spread(0)
-    for cp in gcol:
-        cp.wait_recv()
-    mine = grid_row(y, c)
-    part = gsum[pl.ds(pl.multiple_of(mine * OWN, OWN), OWN), :].astype(F32)
-    for i in range(7):
-        part = part + g_col[i].astype(F32)
-    gz_src[...] = part.astype(BF)
-    gzs = [remote(gz_src, g_z.at[i - 1], gz_ss.at[i - 1], gz_rs.at[i - 1], zdev(i)) for i in range(1, NZ)]
-    for cp in gzs:
-        cp.start()
-    spread(1)
 
     for cp in gzs:
         cp.wait_recv()
@@ -398,6 +398,7 @@
 
     for cp in back:
         cp.start()
+    spread(1)
     for cp in back + [edges[0][0], edges[1][0]]:
         cp.wait_recv()
 
@@ -433,24 +434,16 @@
         cp.wait()
 
 
-def finish_kernel(factor, cg, fg, out_cg, out_fg, got, wide, fgv, i_sem, o_sem):
-    parts = got.shape[0]
+def finish_kernel(factor, cg, fg, out_cg, out_fg, wide, sem):
+    parts = wide.shape[0]
     rows = CODES // parts
-    take_fg = pltpu.make_async_copy(fg, fgv, i_sem.at[parts])
-    takes, gives = [], []
+    gives = [pltpu.make_async_copy(fg, out_fg, sem.at[parts])]
+    gives[0].start()
     for n in range(parts):
         at = pl.ds(n * rows, rows)
-        takes.append(pltpu.make_async_copy(cg.at[at], got.at[n], i_sem.at[n]))
-        gives.append(pltpu.make_async_copy(wide.at[n], out_cg.at[at], o_sem.at[n]))
-    gives.append(pltpu.make_async_copy(fgv, out_fg, o_sem.at[parts]))
-    for cp in takes + [take_fg]:
-        cp.start()
-    for n in range(parts):
-        takes[n].wait()
-        wide[n] = got[n].astype(F32) * factor
-        gives[n].start()
-    take_fg.wait()
-    gives[parts].start()
+        wide[n] = cg[at, :].astype(F32) * factor
+        gives.append(pltpu.make_async_copy(wide.at[n], out_cg.at[at], sem.at[n]))
+        gives[-1].start()
     for cp in gives:
         cp.wait()
 
@@ -464,16 +457,13 @@
             jax.ShapeDtypeStruct(cg.shape, F32),
             jax.ShapeDtypeStruct(fg.shape, BF),
         ),
-        in_specs=[hbm, hbm],
+        in_specs=[pl.BlockSpec(memory_space=pltpu.VMEM)] * 2,
         out_specs=(hbm, hbm),
         scratch_shapes=[
-            pltpu.VMEM((parts, CODES // parts, HD), BF),
             pltpu.VMEM((parts, CODES // parts, HD), F32),
-            pltpu.VMEM(fg.shape, BF),
-            pltpu.SemaphoreType.DMA((parts + 1,)),
             pltpu.SemaphoreType.DMA((parts + 1,)),
         ],
-        compiler_params=pltpu.CompilerParams(vmem_limit_bytes=56 << 20),
+        compiler_params=pltpu.CompilerParams(vmem_limit_bytes=40 << 20),
         name="widen",
     )(cg, fg)
 
@@ -486,11 +476,11 @@
     cg, fg = pl.pallas_call(
         kernel,
         out_shape=(
-            jax.ShapeDtypeStruct((CODES, HD), BF),
-            jax.ShapeDtypeStruct((IMG, BAND, LW, CIN), BF),
+            pltpu.VMEM((CODES, HD), BF),
+            pltpu.VMEM((IMG, BAND, LW, CIN), BF),
         ),
         in_specs=[hbm] * 4,
-        out_specs=(hbm, pl.BlockSpec(memory_space=pltpu.VMEM)),
+        out_specs=(pl.BlockSpec(memory_space=pltpu.VMEM), pl.BlockSpec(memory_space=pltpu.VMEM)),
         scratch_shapes=[
             vm((BAND + 2, IMG, LW, CIN), BF),
             vm((3, 3, CIN, D), BF),
@@ -527,7 +517,7 @@
             vm((BAND + 2, OWN, D), BF),
         ] + [dma((n,)) for n in sems] + [pltpu.SemaphoreType.REGULAR((2,))],
         compiler_params=pltpu.CompilerParams(
-            collective_id=0, has_side_effects=True, vmem_limit_bytes=56 << 20
+            collective_id=0, has_side_effects=True, vmem_limit_bytes=58 << 20
         ),
         cost_estimate=pl.CostEstimate(
             flops=12 * 2**30, bytes_accessed=10 << 20, transcendentals=1 << 21

time: 59.8 us -> 56.1 us (0.938)
  Pallas kernels: 59.1 us -> 55.2 us
    pallas_call x1, Pallas kernels: 56.6 us -> 53.7 us  [on_device(): pl.pallas_call(kernel, out_shape=(pltpu.VMEM((CODES, HD), BF), pltpu.VMEM...]
    pallas_call x1, Pallas kernels: 2.47 us -> 1.47 us  [finish(): pl.pallas_call(functools.partial(finish_kernel, factor), out_shape=(jax.S...]
where the time goes in v5:
time: 56.1 us; the launch traced here: 55.8 us
  Pallas kernels  55.2 us (98%)
  between operations  0.64 us (1%)
    pallas_call x1, Pallas kernels, on_device(): pl.pallas_call(kernel, out_shape=(pltpu.VMEM((CODES, HD), BF), pltpu.VMEM...  53.7 us
    pallas_call x1, Pallas kernels, finish(): pl.pallas_call(functools.partial(finish_kernel, factor), out_shape=(jax.S...  1.47 us

profile of v5, /device:TPU:1, one launch (start us, length us, event | category | flops | bytes accessed | tf_op | source)
XLA Modules:
  0.0 55.8 jit_solution(828706100958568751)
XLA Ops:
  0.6 53.7 %soft_quantize.1 = (bf16[4096,128]{1,0:T(8,128)(2,1)S(1)}, bf16[4,4,16,512]{3,2,1,0:T(8,128)(2,1)S(1)}) custom-call(bf16[4,4,16,512]{3,2,1,0:T(8,128)(2,1)} %feat.1, bf16[3,3,512,256]{3,2,1,0:T(8,128)(2,1)} %cw_hbm.1, f32[4096,256]{1,0:T(8,128)} %cb_hbm.1, bf16[4,4,16,256]{3,2,1,0:T(8,128)(2,1)} %up.1), custom_call_target="tpu_custom_call" | custom-call | flops 12884901888 | bytes 10485760 | tf_op jit(solution)/shard_map/soft_quantize/pallas_call | solution.py:476
  54.4 1.5 %widen.1 = (f32[4096,128]{1,0:T(8,128)}, bf16[4,4,16,512]{3,2,1,0:T(8,128)(2,1)}) custom-call(bf16[4096,128]{1,0:T(8,128)(2,1)S(1)} %get-tuple-element.4.cg, bf16[4,4,16,512]{3,2,1,0:T(8,128)(2,1)S(1)} %get-tuple-element.5.fg), custom_call_target="tpu_custom_call" | custom-call | tf_op jit(solution)/shard_map/widen/pallas_call | solution.py:454

commit v6 on v5

--- a/solution.py
+++ b/solution.py
@@ -291,9 +291,6 @@
         pg[:, both:] = g
         return nn(pg[...], right[...].reshape(4 * ROWS, D))
 
-    share_of = jnp.exp(own_logs - total)
-    gsum[...] = (share_of * (sum_g[...] + (own_mean - inner) * sum_w[...])).T.astype(BF)
-
     def grid_row(y_, c_):
         return (y_ // 2) * 2 + c_
 
@@ -307,7 +304,8 @@
     near_x = (1, NX - 1)
     first, second = slice(0, QTR), slice(QTR, PART)
     ring, direct, summed = [], [], []
-    for h in range(2):
+
+    def send_far(h):
         t = term(2, h).astype(BF)
         for n, half in enumerate((first, second)):
             m = 2 * h + n
@@ -315,6 +313,8 @@
             cp = remote(far.at[m], got_far.at[m], r2_ss.at[m], r2_rs.at[m], xdev(near_x[n]))
             cp.start()
             ring.append(cp)
+
+    def send_near(h):
         for n, (now, later) in enumerate(((second, first), (first, second))):
             m = 2 * h + n
             t = term(near_x[n], h)
@@ -325,11 +325,8 @@
             cp = remote(near.at[m, at], to.at[h, at], rd_ss.at[m], rd_rs.at[m], xdev(near_x[n]))
             cp.start()
             direct.append(cp)
-    for cp in gcol:
-        cp.start()
-    for h in range(2):
-        own[h] = term(0, h)
-    for h in range(2):
+
+    def send_sum(h):
         for n, later in enumerate((first, second)):
             m = 2 * h + n
             ring[m].wait_recv()
@@ -340,6 +337,19 @@
             cp.start()
             summed.append(cp)
 
+    send_far(0)
+    send_near(0)
+    send_far(1)
+    share_of = jnp.exp(own_logs - total)
+    gsum[...] = (share_of * (sum_g[...] + (own_mean - inner) * sum_w[...])).T.astype(BF)
+    for cp in gcol:
+        cp.start()
+    own[0] = term(0, 0)
+    send_sum(0)
+    send_near(1)
+    own[1] = term(0, 1)
+    send_sum(1)
+
     for cp in gcol:
         cp.wait_recv()
     mine = grid_row(y, c)
@@ -351,7 +361,7 @@
     for cp in gzs:
         cp.start()
 
-    out, keep = [], []
+    out, over, keep = [], [], []
 
     def spread(h):
         for n in range(2):
@@ -362,16 +372,27 @@
         fin[h, 0] = jnp.where(d == 0, left, rest)
         fin[h, 1] = jnp.where(d == 0, rest, left)
         place = cg.at[pl.ds(pl.multiple_of(d * HALF + s * BLK + h * PART, PART), PART)]
-        for f in (0, 1):
-            for o in (2, 1, 3, 0):
-                if f or o:
-                    n = h * 8 + f * NX + o
-                    out.append(remote(fin.at[h, f], place, a_ss.at[n], a_rs.at[n], agdev(f, o)))
-                    out[-1].start()
+        n = 8 * h + NX
+        over.append(remote(fin.at[h, 1], place, a_ss.at[n], a_rs.at[n], agdev(1, 0)))
+        over[-1].start()
+        for o in (2, 1, 3):
+            n = 8 * h + o
+            out.append(remote(fin.at[h, 0], place, a_ss.at[n], a_rs.at[n], agdev(0, o)))
+            out[-1].start()
         keep.append(pltpu.make_async_copy(fin.at[h, 0], place, l_sem.at[2 + h]))
         keep[-1].start()
 
+    def relay(h):
+        over[h].wait_recv()
+        place = cg.at[pl.ds(pl.multiple_of((1 - d) * HALF + s * BLK + h * PART, PART), PART)]
+        for o in (2, 1, 3):
+            n = 8 * h + NX + o
+            out.append(remote(place, place, a_ss.at[n], a_rs.at[n], agdev(0, o)))
+            out[-1].start()
+
     spread(0)
+    spread(1)
+    relay(0)
 
     for cp in gzs:
         cp.wait_recv()
@@ -398,7 +419,7 @@
 
     for cp in back:
         cp.start()
-    spread(1)
+    relay(1)
     for cp in back + [edges[0][0], edges[1][0]]:
         cp.wait_recv()
 
@@ -428,7 +449,7 @@
             for cp in edges[n]:
                 cp.wait_send()
 
-    for cp in halo + give_u + give_t + col + zs + ring + direct + summed + gcol + gzs + back:
+    for cp in halo + give_u + give_t + col + zs + ring + direct + summed + gcol + gzs + back + over:
         cp.wait_send()
     for cp in keep + out:
         cp.wait()

time: 56.1 us -> 53.5 us (0.954)
  Pallas kernels: 55.2 us -> 52.7 us
    pallas_call x1, Pallas kernels: 53.7 us -> 51.2 us  [on_device(): pl.pallas_call(kernel, out_shape=(pltpu.VMEM((CODES, HD), BF), pltpu.VMEM...]
where the time goes in v6:
time: 53.5 us; the launch traced here: 53.3 us
  Pallas kernels  52.7 us (99%)
  between operations  0.64 us (1%)
    pallas_call x1, Pallas kernels, on_device(): pl.pallas_call(kernel, out_shape=(pltpu.VMEM((CODES, HD), BF), pltpu.VMEM...  51.2 us
    pallas_call x1, Pallas kernels, finish(): pl.pallas_call(functools.partial(finish_kernel, factor), out_shape=(jax.S...  1.47 us

profile of v6, /device:TPU:1, one launch (start us, length us, event | category | flops | bytes accessed | tf_op | source)
XLA Modules:
  0.0 53.3 jit_solution(14856043111625406848)
XLA Ops:
  0.6 51.2 %soft_quantize.1 = (bf16[4096,128]{1,0:T(8,128)(2,1)S(1)}, bf16[4,4,16,512]{3,2,1,0:T(8,128)(2,1)S(1)}) custom-call(bf16[4,4,16,512]{3,2,1,0:T(8,128)(2,1)} %feat.1, bf16[3,3,512,256]{3,2,1,0:T(8,128)(2,1)} %cw_hbm.1, f32[4096,256]{1,0:T(8,128)} %cb_hbm.1, bf16[4,4,16,256]{3,2,1,0:T(8,128)(2,1)} %up.1), custom_call_target="tpu_custom_call" | custom-call | flops 12884901888 | bytes 10485760 | tf_op jit(solution)/shard_map/soft_quantize/pallas_call | solution.py:497
  51.9 1.5 %widen.1 = (f32[4096,128]{1,0:T(8,128)}, bf16[4,4,16,512]{3,2,1,0:T(8,128)(2,1)}) custom-call(bf16[4096,128]{1,0:T(8,128)(2,1)S(1)} %get-tuple-element.4.cg, bf16[4,4,16,512]{3,2,1,0:T(8,128)(2,1)S(1)} %get-tuple-element.5.fg), custom_call_target="tpu_custom_call" | custom-call | tf_op jit(solution)/shard_map/widen/pallas_call | solution.py:475

commit v7 on v6

--- a/solution.py
+++ b/solution.py
@@ -21,6 +21,8 @@
 OWN = IMG * LW
 UNIT = OWN // LW
 HD = D // 2
+COL_ORDER = (5, 4, 3, 7, 2, 6, 1)
+Z_ORDER = (4, 3, 5, 2, 6, 1, 7)
 
 
 def nt(a, b):
@@ -96,23 +98,10 @@
     peers.append(dev(s, y, z, 1 - c))
     for who in peers:
         pl.semaphore_signal(barrier, inc=1, device_id=who, device_id_type=MESH)
-    load_cb.start()
-    for cp in load_x + [load_w] + load_u:
+    for cp in load_u + load_x + [load_w, load_cb]:
         cp.start()
-    load_cb.wait()
-
-    @pl.loop(0, HALF // 256)
-    def _(i):
-        rows = pl.ds(pl.multiple_of(i * 256, 256), 256)
-        v = cb[rows, :]
-        h = v.astype(BF)
-        hi[rows, :] = h
-        lo[rows, :] = (v - h.astype(F32)).astype(BF)
-
     pl.semaphore_wait(barrier, len(peers))
 
-    for cp in load_u:
-        cp.wait()
     halo = [
         remote(feat.at[:, BAND - 1], xp.at[0], h_ss.at[0], h_rs.at[0], xdev(1)),
         remote(feat.at[:, 0], xp.at[BAND + 1], h_ss.at[1], h_rs.at[1], xdev(NX - 1)),
@@ -128,7 +117,11 @@
     give_u = [
         share(right, n * 2 * UNIT, 2 * UNIT, quarter + n * 2 * UNIT, u_ss, u_rs, n) for n in range(2)
     ]
-    for cp in halo + give_u:
+    for cp in halo:
+        cp.start()
+    for cp in load_u:
+        cp.wait()
+    for cp in give_u:
         cp.start()
 
     def tell(n, reach):
@@ -176,12 +169,17 @@
     for cp in load_x + [load_w]:
         cp.wait()
     convolve((1, 2))
-    project(0)
+    load_cb.wait()
 
     @pl.loop(0, HALF // 256)
     def _(i):
-        at = pl.ds(pl.multiple_of(i * 256, 256), 256)
-        hi_t[:, at] = hi[at, :].T
+        rows = pl.ds(pl.multiple_of(i * 256, 256), 256)
+        v = cb[rows, :]
+        h = v.astype(BF)
+        hi[rows, :] = h
+        lo[rows, :] = (v - h.astype(F32)).astype(BF)
+
+    project(0)
 
     pl.semaphore_wait(z_sem.at[0], 2)
     tell(1, 2)
@@ -250,8 +248,13 @@
         return jnp.concatenate([p[2:4], p[0:2], p[6:8], p[4:6]], axis=0)
 
     col = [remote(st, st_col.at[i - 1], sc_ss.at[i - 1], sc_rs.at[i - 1], coldev(i)) for i in range(1, 8)]
-    for cp in col:
-        cp.start()
+    for i in COL_ORDER:
+        col[i - 1].start()
+
+    @pl.loop(0, HALF // 256)
+    def _(i):
+        at = pl.ds(pl.multiple_of(i * 256, 256), 256)
+        hi_t[:, at] = hi[at, :].T
 
     own_logs = jnp.concatenate([e[0] for e in ends], axis=1)
     own_mean = jnp.concatenate([e[1] for e in ends], axis=1)
@@ -261,7 +264,6 @@
         wb[rows, :] = w.astype(BF)
         gb[rows, :] = (w * (proj[rows, :] - own_mean)).astype(BF)
     sum_g[...] = nn(hi_t[...], gb[...])
-    sum_w[...] = nn(hi_t[...], wb[...])
 
     for cp in col:
         cp.wait_recv()
@@ -272,8 +274,9 @@
     logs, mean = combine(parts)
     st_z[0] = jnp.concatenate([logs, mean], axis=0)
     zs = [remote(st_z.at[0], st_z.at[i], sz_ss.at[i - 1], sz_rs.at[i - 1], zdev(i)) for i in range(1, NZ)]
-    for cp in zs:
-        cp.start()
+    for i in Z_ORDER:
+        zs[i - 1].start()
+    sum_w[...] = nn(hi_t[...], wb[...])
     for cp in zs:
         cp.wait_recv()
     logs, mean = combine([st_z[i] for i in range(NZ)])
@@ -342,8 +345,8 @@
     send_far(1)
     share_of = jnp.exp(own_logs - total)
     gsum[...] = (share_of * (sum_g[...] + (own_mean - inner) * sum_w[...])).T.astype(BF)
-    for cp in gcol:
-        cp.start()
+    for i in COL_ORDER:
+        gcol[i - 1].start()
     own[0] = term(0, 0)
     send_sum(0)
     send_near(1)
@@ -358,10 +361,30 @@
         part = part + g_col[i].astype(F32)
     gz_src[...] = part.astype(BF)
     gzs = [remote(gz_src, g_z.at[i - 1], gz_ss.at[i - 1], gz_rs.at[i - 1], zdev(i)) for i in range(1, NZ)]
-    for cp in gzs:
-        cp.start()
-
-    out, over, keep = [], [], []
+    for i in Z_ORDER:
+        gzs[i - 1].start()
+
+    out, over, keep, sides_out = [], [], [], {}
+
+    def along(h, b, src, dst):
+        for o in (2, 1, 3) if h and b else (1, NX - 1):
+            n = 8 * h + NX * b + o
+            cp = remote(src, dst, a_ss.at[n], a_rs.at[n], agdev(0, o))
+            cp.start()
+            if h and b:
+                out.append(cp)
+            else:
+                sides_out[h, b, o] = cp
+
+    def pass_on(h, b):
+        for n, o in enumerate(near_x):
+            sides_out[h, b, o].wait_recv()
+            first_row = (d + b) % 2 * HALF + (s + NX - o) % NX * BLK + h * PART + n * QTR
+            half = cg.at[pl.ds(pl.multiple_of(first_row, QTR), QTR)]
+            m = 16 + 4 * h + 2 * b + n
+            out.append(remote(half, half, a_ss.at[m], a_rs.at[m], agdev(0, o)))
+            out[-1].start()
+
 
     def spread(h):
         for n in range(2):
@@ -375,24 +398,19 @@
         n = 8 * h + NX
         over.append(remote(fin.at[h, 1], place, a_ss.at[n], a_rs.at[n], agdev(1, 0)))
         over[-1].start()
-        for o in (2, 1, 3):
-            n = 8 * h + o
-            out.append(remote(fin.at[h, 0], place, a_ss.at[n], a_rs.at[n], agdev(0, o)))
-            out[-1].start()
+        along(h, 0, fin.at[h, 0], place)
         keep.append(pltpu.make_async_copy(fin.at[h, 0], place, l_sem.at[2 + h]))
         keep[-1].start()
 
     def relay(h):
         over[h].wait_recv()
         place = cg.at[pl.ds(pl.multiple_of((1 - d) * HALF + s * BLK + h * PART, PART), PART)]
-        for o in (2, 1, 3):
-            n = 8 * h + NX + o
-            out.append(remote(place, place, a_ss.at[n], a_rs.at[n], agdev(0, o)))
-            out[-1].start()
+        along(h, 1, place, place)
 
     spread(0)
     spread(1)
     relay(0)
+    pass_on(0, 0)
 
     for cp in gzs:
         cp.wait_recv()
@@ -419,7 +437,9 @@
 
     for cp in back:
         cp.start()
+    pass_on(1, 0)
     relay(1)
+    pass_on(0, 1)
     for cp in back + [edges[0][0], edges[1][0]]:
         cp.wait_recv()
 
@@ -449,7 +469,7 @@
             for cp in edges[n]:
                 cp.wait_send()
 
-    for cp in halo + give_u + give_t + col + zs + ring + direct + summed + gcol + gzs + back + over:
+    for cp in halo + give_u + give_t + col + zs + ring + direct + summed + gcol + gzs + back + over + list(sides_out.values()):
         cp.wait_send()
     for cp in keep + out:
         cp.wait()
@@ -493,7 +513,7 @@
     dma = pltpu.SemaphoreType.DMA
     vm = pltpu.VMEM
     hbm = pl.BlockSpec(memory_space=pl.ANY)
-    sems = [12, 2, 2, 2, 2, 8, 8, 7, 7, 7, 7, 4, 4, 4, 4, 4, 4, 16, 16, 7, 7, 7, 7, 3, 3, 8, 2]
+    sems = [12, 2, 2, 2, 2, 8, 8, 7, 7, 7, 7, 4, 4, 4, 4, 4, 4, 24, 24, 7, 7, 7, 7, 3, 3, 8, 2]
     cg, fg = pl.pallas_call(
         kernel,
         out_shape=(

time: 53.5 us -> 51.8 us (0.968)
  the two profiles are of different devices: /device:TPU:1 before, /device:TPU:24 now
where the time goes in v7:
time: 51.8 us; the launch traced here: 51.7 us
  Pallas kernels  51.1 us (99%)
  between operations  0.64 us (1%)
    pallas_call x1, Pallas kernels, on_device(): pl.pallas_call(kernel, out_shape=(pltpu.VMEM((CODES, HD), BF), pltpu.VMEM...  49.6 us
    pallas_call x1, Pallas kernels, finish(): pl.pallas_call(functools.partial(finish_kernel, factor), out_shape=(jax.S...  1.47 us

profile of v7, /device:TPU:24, one launch (start us, length us, event | category | flops | bytes accessed | tf_op | source)
XLA Modules:
  0.0 51.7 jit_solution(4028654972611627785)
XLA Ops:
  0.6 49.6 %soft_quantize.1 = (bf16[4096,128]{1,0:T(8,128)(2,1)S(1)}, bf16[4,4,16,512]{3,2,1,0:T(8,128)(2,1)S(1)}) custom-call(bf16[4,4,16,512]{3,2,1,0:T(8,128)(2,1)} %feat.1, bf16[3,3,512,256]{3,2,1,0:T(8,128)(2,1)} %cw_hbm.1, f32[4096,256]{1,0:T(8,128)} %cb_hbm.1, bf16[4,4,16,256]{3,2,1,0:T(8,128)(2,1)} %up.1), custom_call_target="tpu_custom_call" | custom-call | flops 12884901888 | bytes 10485760 | tf_op jit(solution)/shard_map/soft_quantize/pallas_call | solution.py:517
  50.3 1.5 %widen.1 = (f32[4096,128]{1,0:T(8,128)}, bf16[4,4,16,512]{3,2,1,0:T(8,128)(2,1)}) custom-call(bf16[4096,128]{1,0:T(8,128)(2,1)S(1)} %get-tuple-element.4.cg, bf16[4,4,16,512]{3,2,1,0:T(8,128)(2,1)S(1)} %get-tuple-element.5.fg), custom_call_target="tpu_custom_call" | custom-call | tf_op jit(solution)/shard_map/widen/pallas_call | solution.py:495

commit v8 on v7

--- a/solution.py
+++ b/solution.py
@@ -263,7 +263,6 @@
         w = wts[rows, :] * jnp.exp(mst[i // 2] - own_logs)
         wb[rows, :] = w.astype(BF)
         gb[rows, :] = (w * (proj[rows, :] - own_mean)).astype(BF)
-    sum_g[...] = nn(hi_t[...], gb[...])
 
     for cp in col:
         cp.wait_recv()
@@ -276,6 +275,7 @@
     zs = [remote(st_z.at[0], st_z.at[i], sz_ss.at[i - 1], sz_rs.at[i - 1], zdev(i)) for i in range(1, NZ)]
     for i in Z_ORDER:
         zs[i - 1].start()
+    sum_g[...] = nn(hi_t[...], gb[...])
     sum_w[...] = nn(hi_t[...], wb[...])
     for cp in zs:
         cp.wait_recv()
@@ -341,12 +341,12 @@
             summed.append(cp)
 
     send_far(0)
-    send_near(0)
-    send_far(1)
     share_of = jnp.exp(own_logs - total)
     gsum[...] = (share_of * (sum_g[...] + (own_mean - inner) * sum_w[...])).T.astype(BF)
     for i in COL_ORDER:
         gcol[i - 1].start()
+    send_near(0)
+    send_far(1)
     own[0] = term(0, 0)
     send_sum(0)
     send_near(1)

time: 51.8 us -> 51.1 us (0.986)
  the two profiles are of different devices: /device:TPU:24 before, /device:TPU:1 now
where the time goes in v8:
time: 51.1 us; the launch traced here: 50.4 us
  Pallas kernels  49.8 us (97%)
  between operations  0.64 us (1%)
    pallas_call x1, Pallas kernels, on_device(): pl.pallas_call(kernel, out_shape=(pltpu.VMEM((CODES, HD), BF), pltpu.VMEM...  48.3 us
    pallas_call x1, Pallas kernels, finish(): pl.pallas_call(functools.partial(finish_kernel, factor), out_shape=(jax.S...  1.47 us

profile of v8, /device:TPU:1, one launch (start us, length us, event | category | flops | bytes accessed | tf_op | source)
XLA Modules:
  0.0 50.4 jit_solution(12040426486009756107)
XLA Ops:
  0.6 48.3 %soft_quantize.1 = (bf16[4096,128]{1,0:T(8,128)(2,1)S(1)}, bf16[4,4,16,512]{3,2,1,0:T(8,128)(2,1)S(1)}) custom-call(bf16[4,4,16,512]{3,2,1,0:T(8,128)(2,1)} %feat.1, bf16[3,3,512,256]{3,2,1,0:T(8,128)(2,1)} %cw_hbm.1, f32[4096,256]{1,0:T(8,128)} %cb_hbm.1, bf16[4,4,16,256]{3,2,1,0:T(8,128)(2,1)} %up.1), custom_call_target="tpu_custom_call" | custom-call | flops 12884901888 | bytes 10485760 | tf_op jit(solution)/shard_map/soft_quantize/pallas_call | solution.py:517
  48.9 1.5 %widen.1 = (f32[4096,128]{1,0:T(8,128)}, bf16[4,4,16,512]{3,2,1,0:T(8,128)(2,1)}) custom-call(bf16[4096,128]{1,0:T(8,128)(2,1)S(1)} %get-tuple-element.4.cg, bf16[4,4,16,512]{3,2,1,0:T(8,128)(2,1)S(1)} %get-tuple-element.5.fg), custom_call_target="tpu_custom_call" | custom-call | tf_op jit(solution)/shard_map/widen/pallas_call | solution.py:495

commit v9 on v8

--- a/solution.py
+++ b/solution.py
@@ -490,7 +490,7 @@
 
 
 def finish(cg, fg, factor):
-    parts = 8
+    parts = 4
     hbm = pl.BlockSpec(memory_space=pl.ANY)
     return pl.pallas_call(
         functools.partial(finish_kernel, factor),

time: 51.1 us -> 51.1 us (level)
  no operation moved by 1% of the time
where the time goes in v9:
time: 51.1 us; the launch traced here: 50.4 us
  Pallas kernels  49.7 us (97%)
  between operations  0.64 us (1%)
    pallas_call x1, Pallas kernels, on_device(): pl.pallas_call(kernel, out_shape=(pltpu.VMEM((CODES, HD), BF), pltpu.VMEM...  48.3 us
    pallas_call x1, Pallas kernels, finish(): pl.pallas_call(functools.partial(finish_kernel, factor), out_shape=(jax.S...  1.44 us

profile of v9, /device:TPU:1, one launch (start us, length us, event | category | flops | bytes accessed | tf_op | source)
XLA Modules:
  0.0 50.4 jit_solution(9344578026773487292)
XLA Ops:
  0.6 48.3 %soft_quantize.1 = (bf16[4096,128]{1,0:T(8,128)(2,1)S(1)}, bf16[4,4,16,512]{3,2,1,0:T(8,128)(2,1)S(1)}) custom-call(bf16[4,4,16,512]{3,2,1,0:T(8,128)(2,1)} %feat.1, bf16[3,3,512,256]{3,2,1,0:T(8,128)(2,1)} %cw_hbm.1, f32[4096,256]{1,0:T(8,128)} %cb_hbm.1, bf16[4,4,16,256]{3,2,1,0:T(8,128)(2,1)} %up.1), custom_call_target="tpu_custom_call" | custom-call | flops 12884901888 | bytes 10485760 | tf_op jit(solution)/shard_map/soft_quantize/pallas_call | solution.py:517
  48.9 1.4 %widen.1 = (f32[4096,128]{1,0:T(8,128)}, bf16[4,4,16,512]{3,2,1,0:T(8,128)(2,1)}) custom-call(bf16[4096,128]{1,0:T(8,128)(2,1)S(1)} %get-tuple-element.4.cg, bf16[4,4,16,512]{3,2,1,0:T(8,128)(2,1)S(1)} %get-tuple-element.5.fg), custom_call_target="tpu_custom_call" | custom-call | tf_op jit(solution)/shard_map/widen/pallas_call | solution.py:495
